TPU v7x, 128 devices: a whole 4x4x4 slice. The times are simulated.
128 devices in a mesh: dp: 16 (over y, x), tensor: 8 (over z, core).
Axes of the slice: x: 4, y: 4, z: 4, core: 2. Of those that a mesh axis runs over, the one named last changes fastest.
Arguments:
- activations: bfloat16 [16384, 8192], P('dp', 'tensor'), may hold values from -6 to 6
- out_grad: bfloat16 [16384, 5120], P('dp', 'tensor'), may hold values from -0.119628906 to 0.119628906
- counts: int32 [16], replicated, may hold values from 128 to 1024, as said below
Outputs:
- weight_grad: float32 [8192, 5120], P('dp', 'tensor')
- bias_grad: float32 [5120], P('tensor')
Inputs may be any that keep to these rules, and one draw needn't show every extreme that they name: `counts`: every entry is a multiple of 128; some rank has all 1024 rows live in every draw.
All inputs are finite; a program needn't handle non-finite values.
Results may differ from a plain program's by a relative error of at most 0.0003.
Values may be sent and summed in bfloat16 or wider, within the bound.
No kernel may reach another device: no remote copies, remote signals or barrier semaphores. Data moves between devices by JAX's collectives and lax.ppermute only.
A program may use at most 128 MiB of HBM per device.

v0:
```python
import jax
import jax.numpy as jnp
from jax import lax
from jax.sharding import PartitionSpec as P

BLK = 128


def gather_features(inputs_now):
    return lax.all_gather(inputs_now, "tensor", axis=1, tiled=True)


def per_device(activations, out_grad, counts):
    own_rank = lax.axis_index("dp")
    loads = counts // BLK
    held_blocks = loads[own_rank]
    width = out_grad.shape[1]
    row_index = jnp.arange(out_grad.shape[0], dtype=jnp.int32)
    masked = jnp.where((row_index < held_blocks * BLK)[:, None], out_grad, jnp.zeros_like(out_grad))
    features = gather_features(activations)
    count = features.shape[1] // lax.axis_size("dp") * lax.axis_size("dp")

    def accumulate(block_index, total):
        piece = lax.dynamic_slice(features, (block_index * BLK, 0), (BLK, count))
        grads = lax.dynamic_slice_in_dim(out_grad, block_index * BLK, BLK, 0)
        return total + lax.dot_general(
            piece, grads, (((0,), (0,)), ((), ())), preferred_element_type=jnp.float32
        )

    weight_grad = lax.psum_scatter(
        lax.fori_loop(0, held_blocks, accumulate, jnp.zeros((count, width), jnp.float32)),
        "dp",
        scatter_dimension=0,
        tiled=True,
    )
    column_sums = jnp.sum(masked.astype(jnp.float32), axis=0)
    bias_grad = lax.psum(column_sums, "dp")
    return (weight_grad, bias_grad)


def solution(mesh):
    in_specs = (P("dp", "tensor"), P("dp", "tensor"), P())
    out_specs = (P("dp", "tensor"), P("tensor"))
    return jax.shard_map(
        per_device, mesh=mesh, in_specs=in_specs, out_specs=out_specs, check_vma=False
    )
```

profile of v0, /device:TPU:1, one launch (start us, length us, event | category | flops | bytes accessed | tf_op | source)
XLA Modules:
  0.0 391.6 jit_solution(13972318914946835179)
XLA Ops:
  7.2 0.0 copy-start
  7.2 0.0 all-gather.2.cloned.1.call-start
  7.2 0.7 all-gather.2.cloned.1.call-update
  7.9 0.0 reduce-scatter.2.cloned.1.call-start
  8.0 0.7 and_select_fusion
  8.6 0.6 dynamic_slice.9
  9.2 89.3 %all-gather.2.cloned.1.call-done = bf16[1024,8192]{1,0:T(8,128)(2,1)} async-done(((bf16[1024,1024]{1,0:T(8,128)(2,1)}), bf16[1024,8192]{1,0:T(8,128)(2,1)}) %all-gather.2.cloned.1.call-update) | async-done | bytes 16777232 | tf_op jit(solution)/shard_map/all_gather | solution.py:10
  98.5 8.3 %broadcast_in_dim.15 = f32[8192,640]{1,0:T(8,128)} broadcast(f32[]{:T(128)} %constant.29.clone.1), dimensions={} | broadcast | bytes 20971524 | tf_op jit(solution)/shard_map/broadcast_in_dim | solution.py:31
  106.8 0.0 copy-done
  106.8 55.1 %while.10 = (s32[]{:T(128)}, f32[8192,640]{1,0:T(8,128)}, s32[]{:T(128)}, bf16[1024,8192]{1,0:T(8,128)(2,1)}, bf16[1024,640]{1,0:T(8,128)(2,1)S(1)}, /*index=5*/s32[]{:T(128)}, s32[]{:T(128)}, s32[]{:T(128)}, s32[]{:T(128)}) while((s32[]{:T(128)}, f32[8192,640]{1,0:T(8,128)}, s32[]{:T(128)}, bf16[1024,8192]{1,0:T(8,128)(2,1)}, ...), condition=%wide.region_1.2_spmd, body=%wide.region_0.1_spmd.sunk | while | flops 1347420160 | bytes 44205192 | solution.py:31
  107.5 17.5 %convolution_add_fusion.2 = f32[8192,640]{1,0:T(8,128)} fusion(f32[8192,640]{1,0:T(8,128)} %get-tuple-element.83, bf16[1024,8192]{1,0:T(8,128)(2,1)} %get-tuple-element.94, s32[]{:T(128)S(6)} %select_n.22, bf16[1024,640]{1,0:T(8,128)(2,1)S(1)} %get-tuple-element.95), kind=kOutput, calls=%fused_computation.clone.1 | convolution fusion | flops 1347420160 | bytes 44205056 | tf_op jit(solution)/shard_map/while/body/dot_general | solution.py:26
  125.6 17.5 %convolution_add_fusion.2 = f32[8192,640]{1,0:T(8,128)} fusion(f32[8192,640]{1,0:T(8,128)} %get-tuple-element.83, bf16[1024,8192]{1,0:T(8,128)(2,1)} %get-tuple-element.94, s32[]{:T(128)S(6)} %select_n.22, bf16[1024,640]{1,0:T(8,128)(2,1)S(1)} %get-tuple-element.95), kind=kOutput, calls=%fused_computation.clone.1 | convolution fusion | flops 1347420160 | bytes 44205056 | tf_op jit(solution)/shard_map/while/body/dot_general | solution.py:26
  143.8 17.5 %convolution_add_fusion.2 = f32[8192,640]{1,0:T(8,128)} fusion(f32[8192,640]{1,0:T(8,128)} %get-tuple-element.83, bf16[1024,8192]{1,0:T(8,128)(2,1)} %get-tuple-element.94, s32[]{:T(128)S(6)} %select_n.22, bf16[1024,640]{1,0:T(8,128)(2,1)S(1)} %get-tuple-element.95), kind=kOutput, calls=%fused_computation.clone.1 | convolution fusion | flops 1347420160 | bytes 44205056 | tf_op jit(solution)/shard_map/while/body/dot_general | solution.py:26
  161.9 0.0 reduce-scatter.2.cloned.1.call-update
  162.6 0.3 convert_reduce_fusion
  163.0 119.5 %psum.7 = f32[640]{0:T(1024)} all-reduce(f32[640]{0:T(1024)S(1)} %convert_reduce_fusion), channel_id=1, replica_groups=mesh['dp'=16,'tensor'=8] {'dp'}, use_global_device_ids=true, to_apply=%region_4.5 | all-reduce | flops 640 | bytes 5120 | tf_op jit(solution)/shard_map/psum | solution.py:37
  282.5 102.3 %reduce-scatter.2.cloned.1.call-done = f32[512,640]{1,0:T(8,128)} async-done(((f32[8192,640]{1,0:T(8,128)}), f32[512,640]{1,0:T(8,128)}) %reduce-scatter.2.cloned.1.call-update) | async-done | bytes 1310736 | tf_op jit(solution)/shard_map/reduce_scatter | solution.py:30
  (1 shorter events, 0.0 us)
Async XLA Ops:
  7.2 99.7 %copy-start = (bf16[1024,640]{1,0:T(8,128)(2,1)S(1)}, bf16[1024,640]{1,0:T(8,128)(2,1)}, u32[]{:S(2)}) copy-start(bf16[1024,640]{1,0:T(8,128)(2,1)} %param.6) | copy-start | bytes 3932164
  7.2 91.3 %all-gather.2.cloned.1.call-start = ((), (), s32[]{:S(2)}) async-start(), calls=%async_computation.1 | async-start | bytes 18874368 | tf_op jit(solution)/shard_map/all_gather | solution.py:10
  7.9 376.9 %reduce-scatter.2.cloned.1.call-start = ((), (), s32[]{:S(2)}) async-start(), calls=%async_computation.2 | async-start | bytes 22282240 | tf_op jit(solution)/shard_map/reduce_scatter | solution.py:30
Sparse Core Ops, SparseCore 0:
  9.7 88.7 all-gather.1
  162.1 222.6 reduce-scatter.1
where the time goes:
time: 391 us; the launch traced here: 392 us
  waiting for transfers between devices  192 us (49%)
  blocking collectives  120 us (31%)
  matrix products  52.5 us (13%)
  between operations  14.7 us (4%)
  local copies, waits for them, and re-layouts  8.93 us (2%)
    psum x1, blocking collectives, per_device(): bias_grad = lax.psum(column_sums, 'dp')  120 us
    reduce_scatter x1, waiting for transfers between devices, per_device(): lax.psum_scatter(lax.fori_loop(0, held_blocks, accumulate, jnp.zeros((cou...  102 us
    all_gather x1, waiting for transfers between devices, gather_features(): return lax.all_gather(inputs_now, 'tensor', axis=1, tiled=True)  89.3 us
    dot_general x3, matrix products, accumulate(): lax.dot_general(piece, grads, (((0,), (0,)), ((), ())), preferred_element...  52.5 us
    broadcast_in_dim x1, local copies, waits for them, and re-layouts, per_device(): jnp.zeros((count, width), jnp.float32)  8.33 us
  transfers between devices with their start and end apart: 2, of which 2 were waited for; matrix products, arithmetic and copies ran while one was open for 0% of the time, Pallas kernels for 0%

commit v1 on v0

v1 whole, which is shorter than its diff:
```python
import jax
import jax.numpy as jnp
from jax import lax
from jax.sharding import PartitionSpec as P


def per_device(activations, out_grad, counts):
    own_rank = lax.axis_index("dp")
    row_index = jnp.arange(out_grad.shape[0], dtype=jnp.int32)
    masked = jnp.where((row_index < counts[own_rank])[:, None], out_grad, jnp.zeros_like(out_grad))
    column_sums = jnp.sum(masked.astype(jnp.float32), axis=0)
    bias_grad = lax.psum(column_sums, "dp")
    features = lax.all_gather(activations, "tensor", axis=1, tiled=True)
    partial = lax.dot_general(
        features, masked, (((0,), (0,)), ((), ())), preferred_element_type=jnp.float32
    )
    weight_grad = lax.psum_scatter(partial, "dp", scatter_dimension=0, tiled=True)
    return (weight_grad, bias_grad)


def solution(mesh):
    in_specs = (P("dp", "tensor"), P("dp", "tensor"), P())
    out_specs = (P("dp", "tensor"), P("tensor"))
    return jax.shard_map(
        per_device, mesh=mesh, in_specs=in_specs, out_specs=out_specs, check_vma=False
    )
```

time: 391 us -> 259 us (0.66)
  blocking collectives: 120 us -> 35.1 us
  matrix products: 52.5 us -> 18.8 us
  local copies, waits for them, and re-layouts: 8.93 us -> 3.37 us
  waiting for transfers between devices: 192 us -> 187 us
    psum x1, blocking collectives: 120 us -> 35.1 us  [per_device(): bias_grad = lax.psum(column_sums, 'dp')]
    dot_general x3 -> x1, matrix products: 52.5 us -> 18.8 us  [per_device(): lax.dot_general(features, masked, (((0,), (0,)), ((), ())), preferred_ele...]
    broadcast_in_dim x1 -> x0, local copies, waits for them, and re-layouts: 8.33 us -> none  [per_device(): jnp.zeros((count, width), jnp.float32)]
    reduce_scatter x1, waiting for transfers between devices: 102 us -> 96.9 us  [per_device(): lax.psum_scatter(partial, 'dp', scatter_dimension=0, tiled=True)]
  transfers between devices with their start and end apart: 2 -> 2, of which waited for: 2 -> 2; matrix products, arithmetic and copies ran while one was open for 0% -> 1% of each run, Pallas kernels for 0% -> 0%
where the time goes in v1:
time: 259 us
  waiting for transfers between devices  187 us (72%)
  blocking collectives  35.1 us (14%)
  matrix products  18.8 us (7%)
  between operations  14.1 us (5%)
  local copies, waits for them, and re-layouts  3.37 us (1%)
    reduce_scatter x1, waiting for transfers between devices, per_device(): lax.psum_scatter(partial, 'dp', scatter_dimension=0, tiled=True)  96.9 us
    all_gather x1, waiting for transfers between devices, per_device(): features = lax.all_gather(activations, 'tensor', axis=1, tiled=True)  89.3 us
    psum x1, blocking collectives, per_device(): bias_grad = lax.psum(column_sums, 'dp')  35.1 us
    dot_general x1, matrix products, per_device(): lax.dot_general(features, masked, (((0,), (0,)), ((), ())), preferred_ele...  18.8 us
  transfers between devices with their start and end apart: 2, of which 2 were waited for; matrix products, arithmetic and copies ran while one was open for 1% of the time, Pallas kernels for 0%

profile of v1, /device:TPU:1, one launch (start us, length us, event | category | flops | bytes accessed | tf_op | source)
XLA Modules:
  0.0 259.3 jit_solution(11254469393336825894)
XLA Ops:
  7.2 0.0 copy-start.1
  7.2 0.0 copy-start
  7.2 0.0 all-gather.2.cloned.1.call-start
  7.2 0.7 all-gather.2.cloned.1.call-update
  7.9 0.0 reduce-scatter.2.cloned.1.call-start
  8.0 0.0 copy-done.1
  8.0 0.6 dynamic_slice.3
  8.6 0.6 iota_compare_fusion
  9.2 89.3 %all-gather.2.cloned.1.call-done = bf16[1024,8192]{1,0:T(8,128)(2,1)} async-done(((bf16[1024,1024]{1,0:T(8,128)(2,1)}), bf16[1024,8192]{1,0:T(8,128)(2,1)}) %all-gather.2.cloned.1.call-update) | async-done | bytes 16777232 | tf_op jit(solution)/shard_map/all_gather | solution.py:13
  98.5 0.0 copy-done
  98.5 18.8 %convolution_bitcast_fusion = f32[8192,640]{0,1:T(8,128)} fusion(bf16[1024,8192]{1,0:T(8,128)(2,1)} %all-gather.2.cloned.1.call-done, bf16[1024,640]{1,0:T(8,128)(2,1)S(1)} %copy-done, pred[1024]{0:T(1024)(128)(4,1)S(1)} %iota_compare_fusion), kind=kOutput, calls=%fused_computation | convolution fusion | flops 10738073600 | bytes 39060480 | tf_op jit(solution)/shard_map/dot_general | solution.py:14
  117.3 0.0 reduce-scatter.2.cloned.1.call-update
  117.4 0.3 convert_reduce_fusion
  117.7 35.1 %psum.7 = f32[640]{0:T(1024)} all-reduce(f32[640]{0:T(1024)S(1)} %convert_reduce_fusion), channel_id=1, replica_groups=mesh['dp'=16,'tensor'=8] {'dp'}, use_global_device_ids=true, to_apply=%region_2.3 | all-reduce | flops 640 | bytes 5120 | tf_op jit(solution)/shard_map/psum | solution.py:12
  152.8 96.9 %reduce-scatter.2.cloned.1.call-done = f32[512,640]{0,1:T(8,128)} async-done(((f32[8192,640]{0,1:T(8,128)}), f32[512,640]{0,1:T(8,128)}) %reduce-scatter.2.cloned.1.call-update) | async-done | bytes 1310736 | tf_op jit(solution)/shard_map/reduce_scatter | solution.py:17
  249.7 2.8 %copy.5 = f32[512,640]{1,0:T(8,128)} copy(f32[512,640]{0,1:T(8,128)} %reduce-scatter.2.cloned.1.call-done) | data formatting | bytes 2621440
Async XLA Ops:
  7.2 0.8 copy-start.1
  7.2 91.3 %copy-start = (bf16[1024,640]{1,0:T(8,128)(2,1)S(1)}, bf16[1024,640]{1,0:T(8,128)(2,1)}, u32[]{:S(2)}) copy-start(bf16[1024,640]{1,0:T(8,128)(2,1)} %param.4) | copy-start | bytes 3932164
  7.2 91.3 %all-gather.2.cloned.1.call-start = ((), (), s32[]{:S(2)}) async-start(), calls=%async_computation.1 | async-start | bytes 18874368 | tf_op jit(solution)/shard_map/all_gather | solution.py:13
  7.9 241.8 %reduce-scatter.2.cloned.1.call-start = ((), (), s32[]{:S(2)}) async-start(), calls=%async_computation.2 | async-start | bytes 22282240 | tf_op jit(solution)/shard_map/reduce_scatter | solution.py:17
Sparse Core Ops, SparseCore 0:
  9.7 88.7 all-gather.1
  117.5 132.1 reduce-scatter.1

commit v2 on v1

v2 whole, which is shorter than its diff:
```python
import functools

import jax
import jax.numpy as jnp
from jax import lax
from jax.experimental import pallas as pl
from jax.experimental.pallas import tpu as pltpu
from jax.sharding import PartitionSpec as P

SIDE = 4
LANES = 128
TILE = 16
EXTRA = 2 * TILE
FINE = 2.0**-15
STEPS = 128.0
TOP = 32700.0
AXES = ("dp", "tensor")
PARAMS = pltpu.CompilerParams(vmem_limit_bytes=20 * 1024 * 1024)


def place(y, x, z, c):
    return ((y % SIDE * SIDE + x % SIDE) * SIDE + z % SIDE) * 2 + c % 2


def pairs(move):
    return [
        (place(y, x, z, c), place(*move(y, x, z, c)))
        for y in range(SIDE)
        for x in range(SIDE)
        for z in range(SIDE)
        for c in range(2)
    ]


def to_owner(step):
    def move(y, x, z, c):
        if c == (x + step) % SIDE // 2:
            return y, x + step, z, 0
        return y, x + step + 2, z, 1

    return pairs(move)


TO_OWNER = [to_owner(step) for step in range(2)]
RING_X = pairs(lambda y, x, z, c: (y, x + 1 - 2 * c, z, c))
RING_Z = pairs(lambda y, x, z, c: (y, x, z + 1 - 2 * c, c))
SWAP = pairs(lambda y, x, z, c: (y, x, z, c + 1))
ALONG_Y = [
    [place(y, x, z, c) for y in range(SIDE)] for x in range(SIDE) for z in range(SIDE) for c in range(2)
]


AWAY_Y = [pairs(lambda y, x, z, c, d=d: (y + d, x, z, c)) for d in range(SIDE)]


def send(value, perm):
    return lax.ppermute(value, AXES, perm)


def after(value, *others):
    return lax.optimization_barrier((value, *others))[0]


def scale_of(top):
    return jnp.ceil(jnp.log2(jnp.maximum(top, 2.0**-100) * (1.0 / TOP)) * STEPS)


def pack(total, bias, out, where):
    rows = total.shape[0]
    step = scale_of(jnp.max(jnp.abs(total), axis=0, keepdims=True))
    coded = jnp.round(total * jnp.exp2(step * (-1.0 / STEPS))).astype(jnp.int32)
    out[(*where, slice(0, rows))] = coded.astype(jnp.int16)
    row = lax.broadcasted_iota(jnp.int32, (TILE, LANES), 0)
    steps = jnp.broadcast_to(step, (TILE, LANES))
    if bias is None:
        out[(*where, slice(rows, rows + TILE))] = steps.astype(jnp.int32).astype(jnp.int16)
        return
    bias_step = jnp.broadcast_to(scale_of(jnp.max(jnp.abs(bias), axis=0, keepdims=True)), bias.shape)
    scaled = bias * jnp.exp2(bias_step * (-1.0 / STEPS))
    high = jnp.round(scaled)
    low = jnp.round((scaled - high) * (1.0 / FINE))
    head = jnp.where(row == 0, steps, high)
    tail = jnp.where(row == 0, bias_step, low)
    out[(*where, slice(rows, rows + TILE))] = head.astype(jnp.int32).astype(jnp.int16)
    out[(*where, slice(rows + TILE, rows + EXTRA))] = tail.astype(jnp.int32).astype(jnp.int16)


def wide(message, where, start, rows):
    return message[(*where, slice(start, start + rows))].astype(jnp.int32).astype(jnp.float32)


def unpack(message, where, rows):
    step = wide(message, where, rows, TILE)[0:1]
    return wide(message, where, 0, rows) * jnp.exp2(step * (1.0 / STEPS))


def unpack_bias(message, where, rows):
    high, low = wide(message, where, rows, TILE), wide(message, where, rows + TILE, TILE)
    row = lax.broadcasted_iota(jnp.int32, (TILE, LANES), 0)
    step = jnp.broadcast_to(low[0:1], (TILE, LANES))
    return jnp.where(row == 0, 0.0, (high + low * FINE) * jnp.exp2(step * (1.0 / STEPS)))


def cut(first, halves, activations, *outs):
    half_columns = activations.shape[1] // 2
    for step, out in enumerate(outs):
        start = pl.multiple_of(halves[step] * half_columns + first, LANES)
        out[...] = activations[:, pl.ds(start, out.shape[1])]


def join(near, far, out):
    tokens = near.shape[0]
    out[0:tokens, :] = near[...]
    out[tokens:, :] = far[...]


def mask(count, out_grad, grads):
    tokens, width = out_grad.shape
    row = lax.broadcasted_iota(jnp.int32, (tokens, LANES), 0)
    for number in range(width // LANES):
        span = slice(number * LANES, (number + 1) * LANES)
        masked = jnp.where(row < count[0], out_grad[:, span].astype(jnp.float32), 0.0)
        grads[span, :] = masked.T.astype(jnp.bfloat16)


def multiply(with_bias, table, *refs):
    grads, held, other = refs[:SIDE], refs[SIDE : 2 * SIDE], refs[2 * SIDE : 3 * SIDE]
    out = refs[-1]
    width, tokens = grads[0].shape
    sums_of_rows = None
    if with_bias:
        ones = jnp.ones((TILE, tokens), jnp.bfloat16)
        sums = sum(
            lax.dot_general(ones, g[...], (((1,), (1,)), ((), ())), preferred_element_type=jnp.float32)
            for g in grads
        )
        row = lax.broadcasted_iota(jnp.int32, (TILE, LANES), 0)
        sums_of_rows = jnp.zeros((TILE, LANES), jnp.float32)
        for number in range(width // LANES):
            span = slice(number * LANES, (number + 1) * LANES)
            sums_of_rows = jnp.where(row == number + 1, sums[:, span], sums_of_rows)
    for slot in range(SIDE):
        factors = [
            (ref, start)
            for ref in (held[slot], other[-slot % SIDE])
            for start in (0, tokens)
        ]
        total = sum(
            jnp.dot(g[...], ref[start : start + tokens, :], preferred_element_type=jnp.float32)
            for g, (ref, start) in zip(grads, factors, strict=True)
        )
        for part in range(total.shape[1] // LANES):
            bias = sums_of_rows if part == 0 else None
            pack(total[:, part * LANES : (part + 1) * LANES], bias, out, (table[slot], part))


def reduce(counts, *refs):
    messages, (out, bias_out) = refs[:-2], refs[-2:]
    rows = messages[0].shape[-2] - EXTRA
    at = 0
    for count in counts:
        mine, messages = messages[:count], messages[count:]
        sources = [(m, ()) for m in mine] if count > 1 else [(mine[0], (n,)) for n in range(SIDE)]
        if at == 0:
            bias_out[...] = sum(unpack_bias(m, (*n, 0), rows) for m, n in sources)
        for part in range(mine[0].shape[-3]):
            total = sum(unpack(m, (*n, part), rows) for m, n in sources)
            out[at : at + LANES, :] = total.T
            at += LANES


def whole():
    return pl.BlockSpec(memory_space=pltpu.VMEM)


def scalars():
    return pl.BlockSpec(memory_space=pltpu.SMEM)


def shape(dtype, *dims):
    return jax.ShapeDtypeStruct(dims, dtype)


def kernel(body, out_shape, scalar, *values, scratch=()):
    return pl.pallas_call(
        body,
        out_shape=out_shape,
        in_specs=[scalars()] * (scalar is not None) + [whole()] * len(values),
        out_specs=[whole()] * len(out_shape),
        scratch_shapes=scratch,
        compiler_params=PARAMS,
    )(*([] if scalar is None else [scalar]), *values)


def per_device(activations, out_grad, counts):
    rank, column = lax.axis_index("dp"), lax.axis_index("tensor")
    y, x, z, c = rank // SIDE, rank % SIDE, column // 2, column % 2
    tokens, width = out_grad.shape
    columns = activations.shape[1] // 4
    parts = columns // LANES
    slots = jnp.arange(SIDE)
    owners = (jnp.where(c == 0, z - slots, z + slots) % SIDE).astype(jnp.int32)
    owners_away = ((owners - y) % SIDE).astype(jnp.int32)
    halves = jnp.stack([x % 2, 1 - x % 2]).astype(jnp.int32)

    def cut_columns(first, value):
        out = [shape(value.dtype, tokens, columns)] * 2
        return kernel(functools.partial(cut, first), out, halves, value)

    def to_owners(cuts):
        got = [send(piece, perm) for piece, perm in zip(cuts, TO_OWNER, strict=True)]
        return kernel(join, [shape(got[0].dtype, 2 * tokens, columns)], None, *got)[0]

    def sums(table, grads, held, other, with_bias):
        (message,) = kernel(
            functools.partial(multiply, with_bias),
            [shape(jnp.int16, SIDE, parts, width + EXTRA, LANES)],
            table,
            *grads,
            *held,
            *other,
        )
        return message

    cuts = cut_columns(0, activations)
    (grad,) = kernel(
        mask,
        [shape(jnp.bfloat16, width, tokens)],
        counts[rank].reshape(1),
        after(out_grad, *cuts),
    )
    more = cut_columns(columns, after(activations, *cuts))
    own = [to_owners(cuts)]
    own.append(to_owners([after(piece, own[0]) for piece in more]))
    ring = [[piece, send(piece, RING_Z)] for piece in own]
    other = [[send(piece, SWAP)] for piece in own]
    grads = [grad]
    for step in range(SIDE - 1):
        grads.append(send(after(grads[-1], *own), RING_X))
    for step in (1, 2):
        for run in range(2):
            piece = ring[run][step]
            ring[run].append(send(after(piece, other[run][step - 1]), RING_Z))
            other[run].append(send(piece, SWAP))
    for run in range(2):
        other[run].append(send(ring[run][3], SWAP))
    first = c == 0
    near, far = jnp.where(first, grads[0], grads[2]), jnp.where(first, grads[2], grads[0])
    grads = [near, grads[1], far, grads[3]]
    early = sums(owners_away, grads, ring[0], other[0], True)
    late = sums(owners, grads, [after(ring[1][0], early), *ring[1][1:]], other[1], False)
    messages = [
        [early[0]] + [send(early[d], AWAY_Y[d]) for d in range(1, SIDE)],
        [lax.all_to_all(late, AXES, 0, 0, axis_index_groups=ALONG_Y, tiled=True)],
    ]
    weight_grad, bias = kernel(
        functools.partial(reduce, tuple(map(len, messages))),
        [shape(jnp.float32, 2 * columns, width), shape(jnp.float32, TILE, LANES)],
        None,
        *messages[0],
        *messages[1],
    )
    return weight_grad, bias[1 : 1 + width // LANES].reshape(width)


def solution(mesh):
    in_specs = (P("dp", "tensor"), P("dp", "tensor"), P())
    out_specs = (P("dp", "tensor"), P("tensor"))
    return jax.shard_map(
        per_device, mesh=mesh, in_specs=in_specs, out_specs=out_specs, check_vma=False
    )
```

time: 259 us -> 167 us (0.64)
  waiting for transfers between devices: 187 us -> 82.5 us
  starting transfers between devices: 0.08 us -> 49.1 us
  blocking collectives: 35.1 us -> 0 us
  Pallas kernels: 0 us -> 24.8 us
  matrix products: 18.8 us -> 0 us
  between operations: 14.1 us -> 0.89 us
  local copies, waits for them, and re-layouts: 3.37 us -> 7.27 us
    reduce_scatter x1 -> x0, waiting for transfers between devices: 96.9 us -> none  [per_device(): lax.psum_scatter(partial, 'dp', scatter_dimension=0, tiled=True)]
    all_gather x1 -> x0, waiting for transfers between devices: 89.3 us -> none  [per_device(): features = lax.all_gather(activations, 'tensor', axis=1, tiled=True)]
    ppermute x0 -> x24, waiting for transfers between devices: none -> 82.5 us  [send(): return lax.ppermute(value, AXES, perm)]
    ppermute x0 -> x24, starting transfers between devices: none -> 44.9 us  [send(): return lax.ppermute(value, AXES, perm)]
    psum x1 -> x0, blocking collectives: 35.1 us -> none  [per_device(): bias_grad = lax.psum(column_sums, 'dp')]
    pallas_call x0 -> x8, Pallas kernels: none -> 24.8 us  [kernel(): pl.pallas_call(body, out_shape=out_shape, in_specs=[scalars()] * (scalar...]
    dot_general x1 -> x0, matrix products: 18.8 us -> none  [per_device(): lax.dot_general(features, masked, (((0,), (0,)), ((), ())), preferred_ele...]
    all_to_all x0 -> x1, starting transfers between devices: none -> 4.19 us  [per_device(): lax.all_to_all(late, AXES, 0, 0, axis_index_groups=ALONG_Y, tiled=True)]
  transfers between devices with their start and end apart: 2 -> 25, of which waited for: 2 -> 12; matrix products, arithmetic and copies ran while one was open for 1% -> 2% of each run, Pallas kernels for 0% -> 7%
where the time goes in v2:
time: 167 us
  waiting for transfers between devices  82.5 us (49%)
  starting transfers between devices  49.1 us (29%)
  Pallas kernels  24.8 us (15%)
  local copies, waits for them, and re-layouts  7.27 us (4%)
  other arithmetic  2.13 us (1%)
    ppermute x24, waiting for transfers between devices, send(): return lax.ppermute(value, AXES, perm)  82.5 us
    ppermute x24, starting transfers between devices, send(): return lax.ppermute(value, AXES, perm)  44.9 us
    pallas_call x8, Pallas kernels, kernel(): pl.pallas_call(body, out_shape=out_shape, in_specs=[scalars()] * (scalar...  24.8 us
    unnamed x30, local copies, waits for them, and re-layouts  6 us
    all_to_all x1, starting transfers between devices, per_device(): lax.all_to_all(late, AXES, 0, 0, axis_index_groups=ALONG_Y, tiled=True)  4.19 us
  transfers between devices with their start and end apart: 25, of which 12 were waited for; matrix products, arithmetic and copies ran while one was open for 2% of the time, Pallas kernels for 7%

profile of v2, /device:TPU:1, one launch (start us, length us, event | category | flops | bytes accessed | tf_op | source)
XLA Modules:
  0.0 166.6 jit_solution(4438906797951035987)
XLA Ops:
  0.7 0.1 pad_add_fusion.halves
  0.7 1.6 copy-done
  2.3 0.7 shard_map.50
  3.0 5.5 %collective-permute-start = (bf16[1024,256]{1,0:T(8,128)(2,1)S(1)}, bf16[1024,256]{1,0:T(8,128)(2,1)S(1)}, u32[]{:S(2)}, u32[]{:S(2)}) collective-permute-start(bf16[1024,256]{1,0:T(8,128)(2,1)S(1)} %get-tuple-element.20), channel_id=1, source_target_pairs={{0,0},{1,17},{2,2},{3,19},{4,4},{5,21},{6,6},{7,23},{8,8},{9,25},{... | collective-permute-start | bytes 1572872 | tf_op jit(solution)/shard_map/ppermute | solution.py:57
  8.5 0.5 collective-permute-start.1
  9.0 0.7 shard_map.53
  9.7 10.2 %collective-permute-done.near = bf16[1024,256]{1,0:T(8,128)(2,1)S(1)} collective-permute-done((bf16[1024,256]{1,0:T(8,128)(2,1)S(1)}, bf16[1024,256]{1,0:T(8,128)(2,1)S(1)}, u32[]{:S(2)}, u32[]{:S(2)}) %collective-permute-start) | collective-permute-done | bytes 524320 | tf_op jit(solution)/shard_map/ppermute | solution.py:57
  19.9 1.4 collective-permute-done.1.far
  21.3 0.1 shard_map.52.refs_4_
  21.4 0.0 copy-start.14
  21.4 0.0 copy-start.9
  21.4 3.7 %collective-permute-start.2 = (bf16[1024,256]{1,0:T(8,128)(2,1)S(1)}, bf16[1024,256]{1,0:T(8,128)(2,1)S(1)}, u32[]{:S(2)}, u32[]{:S(2)}) collective-permute-start(bf16[1024,256]{1,0:T(8,128)(2,1)S(1)} %get-tuple-element.25), channel_id=1, source_target_pairs={{0,0},{1,17},{2,2},{3,19},{4,4},{5,21},{6,6},{7,23},{8,8},{9,25},{... | collective-permute-start | bytes 1572872 | tf_op jit(solution)/shard_map/ppermute | solution.py:57
  25.1 0.6 collective-permute-start.3
  25.6 3.8 %collective-permute-start.7 = (bf16[2048,256]{1,0:T(8,128)(2,1)S(1)}, bf16[2048,256]{1,0:T(8,128)(2,1)}, u32[]{:S(2)}, u32[]{:S(2)}) collective-permute-start(bf16[2048,256]{1,0:T(8,128)(2,1)S(1)} %shard_map.52.refs_4_), channel_id=1, source_target_pairs={{0,2},{1,7},{2,4},{3,1},{4,6},{5,3},{6,0},{7,5},{8,10},{9,15},{10,... | collective-permute-start | bytes 3145736 | tf_op jit(solution)/shard_map/ppermute | solution.py:57
  29.4 0.0 collective-permute-start.8
  29.4 7.7 %collective-permute-done.2.near = bf16[1024,256]{1,0:T(8,128)(2,1)S(1)} collective-permute-done((bf16[1024,256]{1,0:T(8,128)(2,1)S(1)}, bf16[1024,256]{1,0:T(8,128)(2,1)S(1)}, u32[]{:S(2)}, u32[]{:S(2)}) %collective-permute-start.2) | collective-permute-done | bytes 524320 | tf_op jit(solution)/shard_map/ppermute | solution.py:57
  37.1 1.6 collective-permute-done.3.far
  38.7 0.1 shard_map.54.refs_4_
  38.8 3.7 %collective-permute-start.17 = (bf16[2048,256]{1,0:T(8,128)(2,1)S(1)}, bf16[2048,256]{1,0:T(8,128)(2,1)}, u32[]{:S(2)}, u32[]{:S(2)}) collective-permute-start(bf16[2048,256]{1,0:T(8,128)(2,1)S(1)} %shard_map.54.refs_4_), channel_id=1, source_target_pairs={{0,2},{1,7},{2,4},{3,1},{4,6},{5,3},{6,0},{7,5},{8,10},{9,15},{10,... | collective-permute-start | bytes 3145736 | tf_op jit(solution)/shard_map/ppermute | solution.py:57
  42.5 0.0 collective-permute-start.18
  42.5 0.6 dynamic_slice.3.count
  43.1 1.2 shard_map.51
  44.3 0.0 copy-start.4
  44.3 1.9 %collective-permute-start.4 = (bf16[640,1024]{1,0:T(8,128)(2,1)S(1)}, bf16[640,1024]{1,0:T(8,128)(2,1)S(1)}, u32[]{:S(2)}, u32[]{:S(2)}) collective-permute-start(bf16[640,1024]{1,0:T(8,128)(2,1)S(1)} %shard_map.51), channel_id=1, source_target_pairs={{0,8},{1,25},{2,10},{3,27},{4,12},{5,29},{6,14},{7,31},{8,16},{9,1... | collective-permute-start | bytes 3932168 | tf_op jit(solution)/shard_map/ppermute | solution.py:57
  46.2 0.0 collective-permute-done.7.refs_5_
  46.2 0.0 collective-permute-done.8.refs_8_
  46.2 0.2 collective-permute-start.9
  46.4 1.0 collective-permute-start.10
  47.4 6.8 %collective-permute-done.17.refs_5_ = bf16[2048,256]{1,0:T(8,128)(2,1)} collective-permute-done((bf16[2048,256]{1,0:T(8,128)(2,1)S(1)}, bf16[2048,256]{1,0:T(8,128)(2,1)}, u32[]{:S(2)}, u32[]{:S(2)}) %collective-permute-start.17) | collective-permute-done | bytes 1048608 | tf_op jit(solution)/shard_map/ppermute | solution.py:57
  54.3 0.0 collective-permute-done.18.refs_8_
  54.3 3.4 %collective-permute-start.19 = (bf16[2048,256]{1,0:T(8,128)(2,1)}, bf16[2048,256]{1,0:T(8,128)(2,1)}, u32[]{:S(2)}, u32[]{:S(2)}) collective-permute-start(bf16[2048,256]{1,0:T(8,128)(2,1)} %collective-permute-done.17.refs_5_), channel_id=1, source_target_pairs={{0,2},{1,7},{2,4},{3,1},{4,6},{5,3},{6,0},{7,5},{8,10},{9,15},{10,... | collective-permute-start | bytes 3145736 | tf_op jit(solution)/shard_map/ppermute | solution.py:57
  57.7 4.3 %collective-permute-done.4.refs_1_ = bf16[640,1024]{1,0:T(8,128)(2,1)S(1)} collective-permute-done((bf16[640,1024]{1,0:T(8,128)(2,1)S(1)}, bf16[640,1024]{1,0:T(8,128)(2,1)S(1)}, u32[]{:S(2)}, u32[]{:S(2)}) %collective-permute-start.4) | collective-permute-done | bytes 1310752 | tf_op jit(solution)/shard_map/ppermute | solution.py:57
  62.0 2.3 %collective-permute-start.5 = (bf16[640,1024]{1,0:T(8,128)(2,1)S(1)}, bf16[640,1024]{1,0:T(8,128)(2,1)}, u32[]{:S(2)}, u32[]{:S(2)}) collective-permute-start(bf16[640,1024]{1,0:T(8,128)(2,1)S(1)} %collective-permute-done.4.refs_1_), channel_id=1, source_target_pairs={{0,8},{1,25},{2,10},{3,27},{4,12},{5,29},{6,14},{7,31},{8,16},{9,1... | collective-permute-start | bytes 3932168 | tf_op jit(solution)/shard_map/ppermute | solution.py:57
  64.3 1.3 collective-permute-done.9.refs_6_
  65.6 1.0 copy-done.12
  66.6 3.1 %collective-permute-start.11 = (bf16[2048,256]{1,0:T(8,128)(2,1)}, bf16[2048,256]{1,0:T(8,128)(2,1)}, u32[]{:S(2)}, u32[]{:S(2)}) collective-permute-start(bf16[2048,256]{1,0:T(8,128)(2,1)} %collective-permute-done.9.refs_6_), channel_id=1, source_target_pairs={{0,2},{1,7},{2,4},{3,1},{4,6},{5,3},{6,0},{7,5},{8,10},{9,15},{10,... | collective-permute-start | bytes 3145736 | tf_op jit(solution)/shard_map/ppermute | solution.py:57
  69.7 7.1 %collective-permute-done.19.refs_6_ = bf16[2048,256]{1,0:T(8,128)(2,1)} collective-permute-done((bf16[2048,256]{1,0:T(8,128)(2,1)}, bf16[2048,256]{1,0:T(8,128)(2,1)}, u32[]{:S(2)}, u32[]{:S(2)}) %collective-permute-start.19) | collective-permute-done | bytes 1048608 | tf_op jit(solution)/shard_map/ppermute | solution.py:57
  76.8 0.0 collective-permute-done.20.refs_9_
  76.8 1.0 copy-done.10
  77.9 3.4 %collective-permute-start.21 = (bf16[2048,256]{1,0:T(8,128)(2,1)}, bf16[2048,256]{1,0:T(8,128)(2,1)}, u32[]{:S(2)}, u32[]{:S(2)}) collective-permute-start(bf16[2048,256]{1,0:T(8,128)(2,1)} %collective-permute-done.19.refs_6_), channel_id=1, source_target_pairs={{0,2},{1,7},{2,4},{3,1},{4,6},{5,3},{6,0},{7,5},{8,10},{9,15},{10,... | collective-permute-start | bytes 3145736 | tf_op jit(solution)/shard_map/ppermute | solution.py:57
  81.3 1.6 collective-permute-start.6
  82.9 5.2 %collective-permute-done.11.refs_7_ = bf16[2048,256]{1,0:T(8,128)(2,1)} collective-permute-done((bf16[2048,256]{1,0:T(8,128)(2,1)}, bf16[2048,256]{1,0:T(8,128)(2,1)}, u32[]{:S(2)}, u32[]{:S(2)}) %collective-permute-start.11) | collective-permute-done | bytes 1048608 | tf_op jit(solution)/shard_map/ppermute | solution.py:57
  88.1 2.5 %collective-permute-start.13 = (bf16[2048,256]{1,0:T(8,128)(2,1)}, bf16[2048,256]{1,0:T(8,128)(2,1)}, u32[]{:S(2)}, u32[]{:S(2)}) collective-permute-start(bf16[2048,256]{1,0:T(8,128)(2,1)} %collective-permute-done.11.refs_7_), channel_id=1, source_target_pairs={{0,1},{1,0},{2,3},{3,2},{4,5},{5,4},{6,7},{7,6},{8,9},{9,8},{10,11... | collective-permute-start | bytes 3145736 | tf_op jit(solution)/shard_map/ppermute | solution.py:57
  90.6 0.0 collective-permute-start.22
  90.6 8.7 %collective-permute-done.21.refs_7_ = bf16[2048,256]{1,0:T(8,128)(2,1)} collective-permute-done((bf16[2048,256]{1,0:T(8,128)(2,1)}, bf16[2048,256]{1,0:T(8,128)(2,1)}, u32[]{:S(2)}, u32[]{:S(2)}) %collective-permute-start.21) | collective-permute-done | bytes 1048608 | tf_op jit(solution)/shard_map/ppermute | solution.py:57
  99.3 2.5 %collective-permute-start.23 = (bf16[2048,256]{1,0:T(8,128)(2,1)}, bf16[2048,256]{1,0:T(8,128)(2,1)}, u32[]{:S(2)}, u32[]{:S(2)}) collective-permute-start(bf16[2048,256]{1,0:T(8,128)(2,1)} %collective-permute-done.21.refs_7_), channel_id=1, source_target_pairs={{0,1},{1,0},{2,3},{3,2},{4,5},{5,4},{6,7},{7,6},{8,9},{9,8},{10,11... | collective-permute-start | bytes 3145736 | tf_op jit(solution)/shard_map/ppermute | solution.py:57
  101.9 2.0 %broadcast_select_fusion = (bf16[640,1024]{1,0:T(8,128)(2,1)S(1)}, bf16[640,1024]{1,0:T(8,128)(2,1)S(1)}) fusion(bf16[640,1024]{1,0:T(8,128)(2,1)} %collective-permute-done.5, bf16[640,1024]{1,0:T(8,128)(2,1)} %copy-done.4, pred[]{:T(512)S(6)} %eq.12), kind=kLoop, calls=%fused_computation | loop fusion | flops 1310720 | bytes 5242881 | tf_op jit(solution)/shard_map/jit(_where)/select_n | solution.py:248
  103.9 0.0 collective-permute-done.12.refs_10_
  103.9 0.0 collective-permute-done.13.refs_11_
  103.9 0.0 copy-start.1
  104.0 1.0 copy-done.1
  105.0 1.3 copy-done.2
  106.3 10.3 %shard_map.55 = s16[4,2,672,128]{3,2,1,0:T(8,128)(2,1)S(1)} custom-call(s32[4]{0:T(128)S(1)} %get-tuple-element.38.table, bf16[640,1024]{1,0:T(8,128)(2,1)S(1)} %get-tuple-element.41.refs_0_, bf16[640,1024]{1,0:T(8,128)(2,1)S(1)} %collective-permute-done.4.refs_1_, bf16[640,1024]{1,0:T(8,128)(2,1)S(1)} %get-tuple-element.40.refs_2_, ...), custom_call_target="tpu_custom_call" | custom-call | tf_op jit(solution)/shard_map/pallas_call | solution.py:185
  116.7 0.0 collective-permute-done.23.refs_11_
  116.7 10.0 %shard_map.56 = s16[4,2,672,128]{3,2,1,0:T(8,128)(2,1)} custom-call(s32[4]{0:T(128)S(1)} %get-tuple-element.39.table, bf16[640,1024]{1,0:T(8,128)(2,1)S(1)} %get-tuple-element.41.refs_0_, bf16[640,1024]{1,0:T(8,128)(2,1)S(1)} %collective-permute-done.4.refs_1_, bf16[640,1024]{1,0:T(8,128)(2,1)S(1)} %get-tuple-element.40.refs_2_, ...), custom_call_target="tpu_custom_call" | custom-call | tf_op jit(solution)/shard_map/pallas_call | solution.py:185
  126.7 4.2 %all-to-all-start = ((s16[4,2,672,128]{3,2,1,0:T(8,128)(2,1)}), s16[4,2,672,128]{3,2,1,0:T(8,128)(2,1)S(1)}, u32[]{:S(2)}, u32[]{:S(2)}) async-start(s16[4,2,672,128]{3,2,1,0:T(8,128)(2,1)} %shard_map.56), calls=%async_computation | async-start | bytes 2752512 | tf_op jit(solution)/shard_map/all_to_all | solution.py:254
  130.9 0.1 slice_bitcast_fusion
  131.0 1.5 collective-permute-start.14
  132.5 2.4 %collective-permute-start.15 = (s16[2,672,128]{2,1,0:T(8,128)(2,1)S(1)}, s16[2,672,128]{2,1,0:T(8,128)(2,1)S(1)}, u32[]{:S(2)}, u32[]{:S(2)}) collective-permute-start(s16[2,672,128]{2,1,0:T(8,128)(2,1)S(1)} %get-tuple-element.43), channel_id=1, source_target_pairs={{0,64},{1,65},{2,66},{3,67},{4,68},{5,69},{6,70},{7,71},{8,72},{9,... | collective-permute-start | bytes 1032200 | tf_op jit(solution)/shard_map/ppermute | solution.py:57
  134.9 1.2 collective-permute-start.16
  136.1 20.3 %collective-permute-done.14.refs_1_ = s16[2,672,128]{2,1,0:T(8,128)(2,1)S(1)} collective-permute-done((s16[2,672,128]{2,1,0:T(8,128)(2,1)S(1)}, s16[2,672,128]{2,1,0:T(8,128)(2,1)S(1)}, u32[]{:S(2)}, u32[]{:S(2)}) %collective-permute-start.14) | collective-permute-done | bytes 344096 | tf_op jit(solution)/shard_map/ppermute | solution.py:57
  156.5 7.7 %collective-permute-done.15.refs_2_ = s16[2,672,128]{2,1,0:T(8,128)(2,1)S(1)} collective-permute-done((s16[2,672,128]{2,1,0:T(8,128)(2,1)S(1)}, s16[2,672,128]{2,1,0:T(8,128)(2,1)S(1)}, u32[]{:S(2)}, u32[]{:S(2)}) %collective-permute-start.15) | collective-permute-done | bytes 344096 | tf_op jit(solution)/shard_map/ppermute | solution.py:57
  164.2 1.8 %shard_map.57 = (f32[512,640]{1,0:T(8,128)}, f32[16,128]{1,0:T(8,128)S(1)}) custom-call(s16[2,672,128]{2,1,0:T(8,128)(2,1)S(1)} %get-tuple-element.45.refs_0_, s16[2,672,128]{2,1,0:T(8,128)(2,1)S(1)} %collective-permute-done.14.refs_1_, s16[2,672,128]{2,1,0:T(8,128)(2,1)S(1)} %collective-permute-done.15.refs_2_, ...), custom_call_target="tpu_custom_call" | custom-call | tf_op jit(solution)/shard_map/pallas_call | solution.py:185
  166.0 0.6 slice_bitcast_fusion.4
  (30 shorter events, 0.1 us)
Async XLA Ops:
  0.7 1.6 copy-start
  3.0 16.9 %collective-permute-start = (bf16[1024,256]{1,0:T(8,128)(2,1)S(1)}, bf16[1024,256]{1,0:T(8,128)(2,1)S(1)}, u32[]{:S(2)}, u32[]{:S(2)}) collective-permute-start(bf16[1024,256]{1,0:T(8,128)(2,1)S(1)} %get-tuple-element.20), channel_id=1, source_target_pairs={{0,0},{1,17},{2,2},{3,19},{4,4},{5,21},{6,6},{7,23},{8,8},{9,25},{... | collective-permute-start | bytes 1572872 | tf_op jit(solution)/shard_map/ppermute | solution.py:57
  8.5 12.8 %collective-permute-start.1 = (bf16[1024,256]{1,0:T(8,128)(2,1)S(1)}, bf16[1024,256]{1,0:T(8,128)(2,1)S(1)}, u32[]{:S(2)}, u32[]{:S(2)}) collective-permute-start(bf16[1024,256]{1,0:T(8,128)(2,1)S(1)} %get-tuple-element.21), channel_id=1, source_target_pairs={{0,8},{1,25},{2,10},{3,27},{4,12},{5,29},{6,14},{7,31},{8,1},{9,16... | collective-permute-start | bytes 1572872 | tf_op jit(solution)/shard_map/ppermute | solution.py:57
  21.3 22.9 %copy-start.5 = (bf16[2048,256]{1,0:T(8,128)(2,1)}, bf16[2048,256]{1,0:T(8,128)(2,1)S(1)}, u32[]{:S(2)}) copy-start(bf16[2048,256]{1,0:T(8,128)(2,1)S(1)} %shard_map.52.refs_4_) | copy-start | bytes 3145732
  21.4 21.2 %copy-start.14 = (s32[16]{0:T(128)S(1)}, s32[16]{0:T(128)}, u32[]{:S(2)}) copy-start(s32[16]{0:T(128)} %param.5) | copy-start | bytes 196
  21.4 21.7 %copy-start.9 = (bf16[1024,640]{1,0:T(8,128)(2,1)S(1)}, bf16[1024,640]{1,0:T(8,128)(2,1)}, u32[]{:S(2)}) copy-start(bf16[1024,640]{1,0:T(8,128)(2,1)} %out_grad) | copy-start | bytes 3932164
  21.4 15.7 %collective-permute-start.2 = (bf16[1024,256]{1,0:T(8,128)(2,1)S(1)}, bf16[1024,256]{1,0:T(8,128)(2,1)S(1)}, u32[]{:S(2)}, u32[]{:S(2)}) collective-permute-start(bf16[1024,256]{1,0:T(8,128)(2,1)S(1)} %get-tuple-element.25), channel_id=1, source_target_pairs={{0,0},{1,17},{2,2},{3,19},{4,4},{5,21},{6,6},{7,23},{8,8},{9,25},{... | collective-permute-start | bytes 1572872 | tf_op jit(solution)/shard_map/ppermute | solution.py:57
  25.1 13.7 %collective-permute-start.3 = (bf16[1024,256]{1,0:T(8,128)(2,1)S(1)}, bf16[1024,256]{1,0:T(8,128)(2,1)S(1)}, u32[]{:S(2)}, u32[]{:S(2)}) collective-permute-start(bf16[1024,256]{1,0:T(8,128)(2,1)S(1)} %get-tuple-element.27), channel_id=1, source_target_pairs={{0,8},{1,25},{2,10},{3,27},{4,12},{5,29},{6,14},{7,31},{8,1},{9,16... | collective-permute-start | bytes 1572872 | tf_op jit(solution)/shard_map/ppermute | solution.py:57
  25.6 20.6 %collective-permute-start.7 = (bf16[2048,256]{1,0:T(8,128)(2,1)S(1)}, bf16[2048,256]{1,0:T(8,128)(2,1)}, u32[]{:S(2)}, u32[]{:S(2)}) collective-permute-start(bf16[2048,256]{1,0:T(8,128)(2,1)S(1)} %shard_map.52.refs_4_), channel_id=1, source_target_pairs={{0,2},{1,7},{2,4},{3,1},{4,6},{5,3},{6,0},{7,5},{8,10},{9,15},{10,... | collective-permute-start | bytes 3145736 | tf_op jit(solution)/shard_map/ppermute | solution.py:57
  29.4 16.9 %collective-permute-start.8 = (bf16[2048,256]{1,0:T(8,128)(2,1)S(1)}, bf16[2048,256]{1,0:T(8,128)(2,1)}, u32[]{:S(2)}, u32[]{:S(2)}) collective-permute-start(bf16[2048,256]{1,0:T(8,128)(2,1)S(1)} %shard_map.52.refs_4_), channel_id=1, source_target_pairs={{0,1},{1,0},{2,3},{3,2},{4,5},{5,4},{6,7},{7,6},{8,9},{9,8},{10,11... | collective-permute-start | bytes 3145736 | tf_op jit(solution)/shard_map/ppermute | solution.py:57
  38.8 5.5 %copy-start.7 = (bf16[2048,256]{1,0:T(8,128)(2,1)}, bf16[2048,256]{1,0:T(8,128)(2,1)S(1)}, u32[]{:S(2)}) copy-start(bf16[2048,256]{1,0:T(8,128)(2,1)S(1)} %shard_map.54.refs_4_) | copy-start | bytes 3145732
  38.8 15.5 %collective-permute-start.17 = (bf16[2048,256]{1,0:T(8,128)(2,1)S(1)}, bf16[2048,256]{1,0:T(8,128)(2,1)}, u32[]{:S(2)}, u32[]{:S(2)}) collective-permute-start(bf16[2048,256]{1,0:T(8,128)(2,1)S(1)} %shard_map.54.refs_4_), channel_id=1, source_target_pairs={{0,2},{1,7},{2,4},{3,1},{4,6},{5,3},{6,0},{7,5},{8,10},{9,15},{10,... | collective-permute-start | bytes 3145736 | tf_op jit(solution)/shard_map/ppermute | solution.py:57
  42.5 11.7 %collective-permute-start.18 = (bf16[2048,256]{1,0:T(8,128)(2,1)S(1)}, bf16[2048,256]{1,0:T(8,128)(2,1)}, u32[]{:S(2)}, u32[]{:S(2)}) collective-permute-start(bf16[2048,256]{1,0:T(8,128)(2,1)S(1)} %shard_map.54.refs_4_), channel_id=1, source_target_pairs={{0,1},{1,0},{2,3},{3,2},{4,5},{5,4},{6,7},{7,6},{8,9},{9,8},{10,11... | collective-permute-start | bytes 3145736 | tf_op jit(solution)/shard_map/ppermute | solution.py:57
  44.3 37.0 %copy-start.4 = (bf16[640,1024]{1,0:T(8,128)(2,1)}, bf16[640,1024]{1,0:T(8,128)(2,1)S(1)}, u32[]{:S(2)}) copy-start(bf16[640,1024]{1,0:T(8,128)(2,1)S(1)} %shard_map.51) | copy-start | bytes 3932164
  44.3 17.7 %collective-permute-start.4 = (bf16[640,1024]{1,0:T(8,128)(2,1)S(1)}, bf16[640,1024]{1,0:T(8,128)(2,1)S(1)}, u32[]{:S(2)}, u32[]{:S(2)}) collective-permute-start(bf16[640,1024]{1,0:T(8,128)(2,1)S(1)} %shard_map.51), channel_id=1, source_target_pairs={{0,8},{1,25},{2,10},{3,27},{4,12},{5,29},{6,14},{7,31},{8,16},{9,1... | collective-permute-start | bytes 3932168 | tf_op jit(solution)/shard_map/ppermute | solution.py:57
  46.2 19.4 %collective-permute-start.9 = (bf16[2048,256]{1,0:T(8,128)(2,1)}, bf16[2048,256]{1,0:T(8,128)(2,1)}, u32[]{:S(2)}, u32[]{:S(2)}) collective-permute-start(bf16[2048,256]{1,0:T(8,128)(2,1)} %collective-permute-done.7.refs_5_), channel_id=1, source_target_pairs={{0,2},{1,7},{2,4},{3,1},{4,6},{5,3},{6,0},{7,5},{8,10},{9,15},{10,... | collective-permute-start | bytes 3145736 | tf_op jit(solution)/shard_map/ppermute | solution.py:57
  46.4 19.2 %collective-permute-start.10 = (bf16[2048,256]{1,0:T(8,128)(2,1)}, bf16[2048,256]{1,0:T(8,128)(2,1)S(1)}, u32[]{:S(2)}, u32[]{:S(2)}) collective-permute-start(bf16[2048,256]{1,0:T(8,128)(2,1)} %collective-permute-done.7.refs_5_), channel_id=1, source_target_pairs={{0,1},{1,0},{2,3},{3,2},{4,5},{5,4},{6,7},{7,6},{8,9},{9,8},{10,11... | collective-permute-start | bytes 3145736 | tf_op jit(solution)/shard_map/ppermute | solution.py:57
  54.3 22.6 %collective-permute-start.19 = (bf16[2048,256]{1,0:T(8,128)(2,1)}, bf16[2048,256]{1,0:T(8,128)(2,1)}, u32[]{:S(2)}, u32[]{:S(2)}) collective-permute-start(bf16[2048,256]{1,0:T(8,128)(2,1)} %collective-permute-done.17.refs_5_), channel_id=1, source_target_pairs={{0,2},{1,7},{2,4},{3,1},{4,6},{5,3},{6,0},{7,5},{8,10},{9,15},{10,... | collective-permute-start | bytes 3145736 | tf_op jit(solution)/shard_map/ppermute | solution.py:57
  57.7 19.2 %collective-permute-start.20 = (bf16[2048,256]{1,0:T(8,128)(2,1)}, bf16[2048,256]{1,0:T(8,128)(2,1)S(1)}, u32[]{:S(2)}, u32[]{:S(2)}) collective-permute-start(bf16[2048,256]{1,0:T(8,128)(2,1)} %collective-permute-done.17.refs_5_), channel_id=1, source_target_pairs={{0,1},{1,0},{2,3},{3,2},{4,5},{5,4},{6,7},{7,6},{8,9},{9,8},{10,11... | collective-permute-start | bytes 3145736 | tf_op jit(solution)/shard_map/ppermute | solution.py:57
  62.0 19.3 %collective-permute-start.5 = (bf16[640,1024]{1,0:T(8,128)(2,1)S(1)}, bf16[640,1024]{1,0:T(8,128)(2,1)}, u32[]{:S(2)}, u32[]{:S(2)}) collective-permute-start(bf16[640,1024]{1,0:T(8,128)(2,1)S(1)} %collective-permute-done.4.refs_1_), channel_id=1, source_target_pairs={{0,8},{1,25},{2,10},{3,27},{4,12},{5,29},{6,14},{7,31},{8,16},{9,1... | collective-permute-start | bytes 3932168 | tf_op jit(solution)/shard_map/ppermute | solution.py:57
  65.6 1.0 copy-start.12
  66.6 21.5 %collective-permute-start.11 = (bf16[2048,256]{1,0:T(8,128)(2,1)}, bf16[2048,256]{1,0:T(8,128)(2,1)}, u32[]{:S(2)}, u32[]{:S(2)}) collective-permute-start(bf16[2048,256]{1,0:T(8,128)(2,1)} %collective-permute-done.9.refs_6_), channel_id=1, source_target_pairs={{0,2},{1,7},{2,4},{3,1},{4,6},{5,3},{6,0},{7,5},{8,10},{9,15},{10,... | collective-permute-start | bytes 3145736 | tf_op jit(solution)/shard_map/ppermute | solution.py:57
  76.8 1.0 copy-start.10
  77.9 21.4 %collective-permute-start.21 = (bf16[2048,256]{1,0:T(8,128)(2,1)}, bf16[2048,256]{1,0:T(8,128)(2,1)}, u32[]{:S(2)}, u32[]{:S(2)}) collective-permute-start(bf16[2048,256]{1,0:T(8,128)(2,1)} %collective-permute-done.19.refs_6_), channel_id=1, source_target_pairs={{0,2},{1,7},{2,4},{3,1},{4,6},{5,3},{6,0},{7,5},{8,10},{9,15},{10,... | collective-permute-start | bytes 3145736 | tf_op jit(solution)/shard_map/ppermute | solution.py:57
  81.3 22.7 %collective-permute-start.6 = (bf16[640,1024]{1,0:T(8,128)(2,1)}, bf16[640,1024]{1,0:T(8,128)(2,1)S(1)}, u32[]{:S(2)}, u32[]{:S(2)}) collective-permute-start(bf16[640,1024]{1,0:T(8,128)(2,1)} %collective-permute-done.5), channel_id=1, source_target_pairs={{0,8},{1,25},{2,10},{3,27},{4,12},{5,29},{6,14},{7,31},{8,16},{9,1... | collective-permute-start | bytes 3932168 | tf_op jit(solution)/shard_map/ppermute | solution.py:57
  82.9 21.1 %collective-permute-start.12 = (bf16[2048,256]{1,0:T(8,128)(2,1)}, bf16[2048,256]{1,0:T(8,128)(2,1)}, u32[]{:S(2)}, u32[]{:S(2)}) collective-permute-start(bf16[2048,256]{1,0:T(8,128)(2,1)} %collective-permute-done.9.refs_6_), channel_id=1, source_target_pairs={{0,1},{1,0},{2,3},{3,2},{4,5},{5,4},{6,7},{7,6},{8,9},{9,8},{10,11... | collective-permute-start | bytes 3145736 | tf_op jit(solution)/shard_map/ppermute | solution.py:57
  88.1 15.9 %collective-permute-start.13 = (bf16[2048,256]{1,0:T(8,128)(2,1)}, bf16[2048,256]{1,0:T(8,128)(2,1)}, u32[]{:S(2)}, u32[]{:S(2)}) collective-permute-start(bf16[2048,256]{1,0:T(8,128)(2,1)} %collective-permute-done.11.refs_7_), channel_id=1, source_target_pairs={{0,1},{1,0},{2,3},{3,2},{4,5},{5,4},{6,7},{7,6},{8,9},{9,8},{10,11... | collective-permute-start | bytes 3145736 | tf_op jit(solution)/shard_map/ppermute | solution.py:57
  90.6 26.0 %collective-permute-start.22 = (bf16[2048,256]{1,0:T(8,128)(2,1)}, bf16[2048,256]{1,0:T(8,128)(2,1)}, u32[]{:S(2)}, u32[]{:S(2)}) collective-permute-start(bf16[2048,256]{1,0:T(8,128)(2,1)} %collective-permute-done.19.refs_6_), channel_id=1, source_target_pairs={{0,1},{1,0},{2,3},{3,2},{4,5},{5,4},{6,7},{7,6},{8,9},{9,8},{10,11... | collective-permute-start | bytes 3145736 | tf_op jit(solution)/shard_map/ppermute | solution.py:57
  99.3 17.4 %collective-permute-start.23 = (bf16[2048,256]{1,0:T(8,128)(2,1)}, bf16[2048,256]{1,0:T(8,128)(2,1)}, u32[]{:S(2)}, u32[]{:S(2)}) collective-permute-start(bf16[2048,256]{1,0:T(8,128)(2,1)} %collective-permute-done.21.refs_7_), channel_id=1, source_target_pairs={{0,1},{1,0},{2,3},{3,2},{4,5},{5,4},{6,7},{7,6},{8,9},{9,8},{10,11... | collective-permute-start | bytes 3145736 | tf_op jit(solution)/shard_map/ppermute | solution.py:57
  101.9 3.1 %copy-start.6 = (bf16[2048,256]{1,0:T(8,128)(2,1)S(1)}, bf16[2048,256]{1,0:T(8,128)(2,1)}, u32[]{:S(2)}) copy-start(bf16[2048,256]{1,0:T(8,128)(2,1)} %copy-done.5) | copy-start | bytes 3145732
  101.9 3.1 %copy-start.13 = (bf16[2048,256]{1,0:T(8,128)(2,1)S(1)}, bf16[2048,256]{1,0:T(8,128)(2,1)}, u32[]{:S(2)}) copy-start(bf16[2048,256]{1,0:T(8,128)(2,1)} %copy-done.12) | copy-start | bytes 3145732
  103.9 1.1 copy-start.1
  105.0 1.3 copy-start.2
  106.3 10.3 %copy-start.3 = (bf16[640,1024]{1,0:T(8,128)(2,1)S(1)}, bf16[640,1024]{1,0:T(8,128)(2,1)}, u32[]{:S(2)}) copy-start(bf16[640,1024]{1,0:T(8,128)(2,1)} %copy-done.1) | copy-start | bytes 3932164
  106.3 10.4 %copy-start.8 = (bf16[2048,256]{1,0:T(8,128)(2,1)S(1)}, bf16[2048,256]{1,0:T(8,128)(2,1)}, u32[]{:S(2)}) copy-start(bf16[2048,256]{1,0:T(8,128)(2,1)} %copy-done.7) | copy-start | bytes 3145732
  106.3 10.4 %copy-start.11 = (bf16[2048,256]{1,0:T(8,128)(2,1)S(1)}, bf16[2048,256]{1,0:T(8,128)(2,1)}, u32[]{:S(2)}) copy-start(bf16[2048,256]{1,0:T(8,128)(2,1)} %copy-done.10) | copy-start | bytes 3145732
  126.7 37.5 %all-to-all-start = ((s16[4,2,672,128]{3,2,1,0:T(8,128)(2,1)}), s16[4,2,672,128]{3,2,1,0:T(8,128)(2,1)S(1)}, u32[]{:S(2)}, u32[]{:S(2)}) async-start(s16[4,2,672,128]{3,2,1,0:T(8,128)(2,1)} %shard_map.56), calls=%async_computation | async-start | bytes 2752512 | tf_op jit(solution)/shard_map/all_to_all | solution.py:254
  131.0 25.5 %collective-permute-start.14 = (s16[2,672,128]{2,1,0:T(8,128)(2,1)S(1)}, s16[2,672,128]{2,1,0:T(8,128)(2,1)S(1)}, u32[]{:S(2)}, u32[]{:S(2)}) collective-permute-start(s16[2,672,128]{2,1,0:T(8,128)(2,1)S(1)} %get-tuple-element.44), channel_id=1, source_target_pairs={{0,32},{1,33},{2,34},{3,35},{4,36},{5,37},{6,38},{7,39},{8,40},{9,... | collective-permute-start | bytes 1032200 | tf_op jit(solution)/shard_map/ppermute | solution.py:57
  132.5 31.6 %collective-permute-start.15 = (s16[2,672,128]{2,1,0:T(8,128)(2,1)S(1)}, s16[2,672,128]{2,1,0:T(8,128)(2,1)S(1)}, u32[]{:S(2)}, u32[]{:S(2)}) collective-permute-start(s16[2,672,128]{2,1,0:T(8,128)(2,1)S(1)} %get-tuple-element.43), channel_id=1, source_target_pairs={{0,64},{1,65},{2,66},{3,67},{4,68},{5,69},{6,70},{7,71},{8,72},{9,... | collective-permute-start | bytes 1032200 | tf_op jit(solution)/shard_map/ppermute | solution.py:57
  134.9 29.2 %collective-permute-start.16 = (s16[2,672,128]{2,1,0:T(8,128)(2,1)S(1)}, s16[2,672,128]{2,1,0:T(8,128)(2,1)S(1)}, u32[]{:S(2)}, u32[]{:S(2)}) collective-permute-start(s16[2,672,128]{2,1,0:T(8,128)(2,1)S(1)} %get-tuple-element.42), channel_id=1, source_target_pairs={{0,96},{1,97},{2,98},{3,99},{4,100},{5,101},{6,102},{7,103},{8,104... | collective-permute-start | bytes 1032200 | tf_op jit(solution)/shard_map/ppermute | solution.py:57

commit v3 on v2

--- a/solution.py
+++ b/solution.py
@@ -45,6 +45,9 @@
 RING_X = pairs(lambda y, x, z, c: (y, x + 1 - 2 * c, z, c))
 RING_Z = pairs(lambda y, x, z, c: (y, x, z + 1 - 2 * c, c))
 SWAP = pairs(lambda y, x, z, c: (y, x, z, c + 1))
+ALONG_X = [
+    [place(y, x, z, c) for x in range(SIDE)] for y in range(SIDE) for z in range(SIDE) for c in range(2)
+]
 ALONG_Y = [
     [place(y, x, z, c) for y in range(SIDE)] for x in range(SIDE) for z in range(SIDE) for c in range(2)
 ]
@@ -55,6 +58,10 @@
 
 def send(value, perm):
     return lax.ppermute(value, AXES, perm)
+
+
+def swap_all(value, groups):
+    return lax.all_to_all(value, AXES, 0, 0, axis_index_groups=groups, tiled=True)
 
 
 def after(value, *others):
@@ -101,10 +108,11 @@
     return jnp.where(row == 0, 0.0, (high + low * FINE) * jnp.exp2(step * (1.0 / STEPS)))
 
 
-def cut(first, halves, activations, *outs):
+def cut(halves, activations, *outs):
     half_columns = activations.shape[1] // 2
-    for step, out in enumerate(outs):
-        start = pl.multiple_of(halves[step] * half_columns + first, LANES)
+    for number, out in enumerate(outs):
+        run, step = number // 2, number % 2
+        start = pl.multiple_of(halves[step] * half_columns + run * out.shape[1], LANES)
         out[...] = activations[:, pl.ds(start, out.shape[1])]
 
 
@@ -120,19 +128,20 @@
     for number in range(width // LANES):
         span = slice(number * LANES, (number + 1) * LANES)
         masked = jnp.where(row < count[0], out_grad[:, span].astype(jnp.float32), 0.0)
-        grads[span, :] = masked.T.astype(jnp.bfloat16)
-
-
-def multiply(with_bias, table, *refs):
-    grads, held, other = refs[:SIDE], refs[SIDE : 2 * SIDE], refs[2 * SIDE : 3 * SIDE]
-    out = refs[-1]
-    width, tokens = grads[0].shape
+        turned = masked.T.astype(jnp.bfloat16)
+        for copy in range(SIDE):
+            grads[copy, span, :] = turned
+
+
+def multiply(with_bias, table, grads, *refs):
+    held, other, out = refs[:SIDE], refs[SIDE : 2 * SIDE], refs[-1]
+    _, width, tokens = grads.shape
     sums_of_rows = None
     if with_bias:
         ones = jnp.ones((TILE, tokens), jnp.bfloat16)
         sums = sum(
-            lax.dot_general(ones, g[...], (((1,), (1,)), ((), ())), preferred_element_type=jnp.float32)
-            for g in grads
+            lax.dot_general(ones, grads[n], (((1,), (1,)), ((), ())), preferred_element_type=jnp.float32)
+            for n in range(SIDE)
         )
         row = lax.broadcasted_iota(jnp.int32, (TILE, LANES), 0)
         sums_of_rows = jnp.zeros((TILE, LANES), jnp.float32)
@@ -140,14 +149,12 @@
             span = slice(number * LANES, (number + 1) * LANES)
             sums_of_rows = jnp.where(row == number + 1, sums[:, span], sums_of_rows)
     for slot in range(SIDE):
-        factors = [
-            (ref, start)
-            for ref in (held[slot], other[-slot % SIDE])
-            for start in (0, tokens)
-        ]
+        factors = [(ref, start) for ref in (held[slot], other[-slot % SIDE]) for start in (0, tokens)]
         total = sum(
-            jnp.dot(g[...], ref[start : start + tokens, :], preferred_element_type=jnp.float32)
-            for g, (ref, start) in zip(grads, factors, strict=True)
+            jnp.dot(
+                grads[table[SIDE + n]], ref[start : start + tokens, :], preferred_element_type=jnp.float32
+            )
+            for n, (ref, start) in enumerate(factors)
         )
         for part in range(total.shape[1] // LANES):
             bias = sums_of_rows if part == 0 else None
@@ -199,16 +206,16 @@
     columns = activations.shape[1] // 4
     parts = columns // LANES
     slots = jnp.arange(SIDE)
-    owners = (jnp.where(c == 0, z - slots, z + slots) % SIDE).astype(jnp.int32)
-    owners_away = ((owners - y) % SIDE).astype(jnp.int32)
+    owners = jnp.where(c == 0, z - slots, z + slots) % SIDE
+    ranks = (x - slots - 2 * c) % SIDE
+    tables = [
+        jnp.concatenate([numbers, ranks]).astype(jnp.int32) for numbers in (owners, (owners - y) % SIDE)
+    ]
     halves = jnp.stack([x % 2, 1 - x % 2]).astype(jnp.int32)
 
-    def cut_columns(first, value):
-        out = [shape(value.dtype, tokens, columns)] * 2
-        return kernel(functools.partial(cut, first), out, halves, value)
-
-    def to_owners(cuts):
+    def to_owners(cuts, *others):
         got = [send(piece, perm) for piece, perm in zip(cuts, TO_OWNER, strict=True)]
+        got[0] = after(got[0], *others)
         return kernel(join, [shape(got[0].dtype, 2 * tokens, columns)], None, *got)[0]
 
     def sums(table, grads, held, other, with_bias):
@@ -216,42 +223,38 @@
             functools.partial(multiply, with_bias),
             [shape(jnp.int16, SIDE, parts, width + EXTRA, LANES)],
             table,
-            *grads,
+            grads,
             *held,
             *other,
         )
         return message
 
-    cuts = cut_columns(0, activations)
+    cuts = kernel(cut, [shape(activations.dtype, tokens, columns)] * 4, halves, activations)
     (grad,) = kernel(
         mask,
-        [shape(jnp.bfloat16, width, tokens)],
+        [shape(jnp.bfloat16, SIDE, width, tokens)],
         counts[rank].reshape(1),
         after(out_grad, *cuts),
     )
-    more = cut_columns(columns, after(activations, *cuts))
-    own = [to_owners(cuts)]
-    own.append(to_owners([after(piece, own[0]) for piece in more]))
+    own = [to_owners(cuts[:2], grad), to_owners(cuts[2:])]
     ring = [[piece, send(piece, RING_Z)] for piece in own]
+    grads = swap_all(after(grad, *own), ALONG_X)
     other = [[send(piece, SWAP)] for piece in own]
-    grads = [grad]
-    for step in range(SIDE - 1):
-        grads.append(send(after(grads[-1], *own), RING_X))
-    for step in (1, 2):
-        for run in range(2):
-            piece = ring[run][step]
-            ring[run].append(send(after(piece, other[run][step - 1]), RING_Z))
-            other[run].append(send(piece, SWAP))
-    for run in range(2):
-        other[run].append(send(ring[run][3], SWAP))
-    first = c == 0
-    near, far = jnp.where(first, grads[0], grads[2]), jnp.where(first, grads[2], grads[0])
-    grads = [near, grads[1], far, grads[3]]
-    early = sums(owners_away, grads, ring[0], other[0], True)
-    late = sums(owners, grads, [after(ring[1][0], early), *ring[1][1:]], other[1], False)
+    ring[0].append(send(ring[0][1], RING_Z))
+    other[0].append(send(ring[0][1], SWAP))
+    ring[1].append(send(after(ring[1][1], other[0][0]), RING_Z))
+    other[1].append(send(ring[1][1], SWAP))
+    ring[0].append(send(after(ring[0][2], other[0][1]), RING_Z))
+    other[0].append(send(ring[0][2], SWAP))
+    ring[1].append(send(after(ring[1][2], *other[1], other[0][2]), RING_Z))
+    other[1].append(send(ring[1][2], SWAP))
+    other[0].append(send(ring[0][3], SWAP))
+    early = sums(tables[0], grads, [after(ring[0][0], ring[1][2]), *ring[0][1:]], other[0], True)
+    other[1].append(send(after(ring[1][3], early), SWAP))
+    late = sums(tables[1], grads, ring[1], other[1], False)
     messages = [
-        [early[0]] + [send(early[d], AWAY_Y[d]) for d in range(1, SIDE)],
-        [lax.all_to_all(late, AXES, 0, 0, axis_index_groups=ALONG_Y, tiled=True)],
+        [swap_all(after(early, ring[1][3]), ALONG_Y)],
+        [late[0]] + [send(late[d], AWAY_Y[d]) for d in range(1, SIDE)],
     ]
     weight_grad, bias = kernel(
         functools.partial(reduce, tuple(map(len, messages))),

time: 167 us -> 158 us (0.946)
  waiting for transfers between devices: 82.5 us -> 65.1 us
  local copies, waits for them, and re-layouts: 7.27 us -> 19.2 us
  starting transfers between devices: 49.1 us -> 44.8 us
  Pallas kernels: 24.8 us -> 26.8 us
  other arithmetic: 2.13 us -> 0.17 us
    ppermute x24 -> x21, waiting for transfers between devices: 82.5 us -> 64.7 us  [send(): return lax.ppermute(value, AXES, perm)]
    unnamed x30 -> x32, local copies, waits for them, and re-layouts: 6 us -> 17.2 us
    ppermute x24 -> x21, starting transfers between devices: 44.9 us -> 35.6 us  [send(): return lax.ppermute(value, AXES, perm)]
    all_to_all x1 -> x2, starting transfers between devices: 4.19 us -> 9.28 us  [swap_all(): lax.all_to_all(value, AXES, 0, 0, axis_index_groups=groups, tiled=True)]
    pallas_call x8 -> x7, Pallas kernels: 24.8 us -> 26.8 us  [kernel(): pl.pallas_call(body, out_shape=out_shape, in_specs=[scalars()] * (scalar...]
    select_n x2 -> x1, other arithmetic: 2.05 us -> 0.02 us  [per_device(): (owners - y) % SIDE]
  transfers between devices with their start and end apart: 25 -> 23, of which waited for: 12 -> 11; matrix products, arithmetic and copies ran while one was open for 2% -> 1% of each run, Pallas kernels for 7% -> 15%
where the time goes in v3:
time: 158 us; the launch traced here: 157 us
  waiting for transfers between devices  65.1 us (41%)
  starting transfers between devices  44.8 us (28%)
  Pallas kernels  26.8 us (17%)
  local copies, waits for them, and re-layouts  19.2 us (12%)
    ppermute x21, waiting for transfers between devices, send(): return lax.ppermute(value, AXES, perm)  64.7 us
    ppermute x21, starting transfers between devices, send(): return lax.ppermute(value, AXES, perm)  35.6 us
    pallas_call x7, Pallas kernels, kernel(): pl.pallas_call(body, out_shape=out_shape, in_specs=[scalars()] * (scalar...  26.8 us
    unnamed x32, local copies, waits for them, and re-layouts  17.2 us
    all_to_all x2, starting transfers between devices, swap_all(): lax.all_to_all(value, AXES, 0, 0, axis_index_groups=groups, tiled=True)  9.28 us
  transfers between devices with their start and end apart: 23, of which 11 were waited for; matrix products, arithmetic and copies ran while one was open for 1% of the time, Pallas kernels for 15%

profile of v3, /device:TPU:1, one launch (start us, length us, event | category | flops | bytes accessed | tf_op | source)
XLA Modules:
  0.0 157.0 jit_solution(8656141442710649024)
XLA Ops:
  0.7 0.1 pad_add_fusion.1.halves
  0.7 1.6 %copy-done.1 = bf16[1024,1024]{1,0:T(8,128)(2,1)S(1)} copy-done((bf16[1024,1024]{1,0:T(8,128)(2,1)S(1)}, bf16[1024,1024]{1,0:T(8,128)(2,1)}, u32[]{:S(2)}) %copy-start.1) | copy-done | bytes 2097176
  2.3 2.2 %shard_map.50 = (bf16[1024,256]{1,0:T(8,128)(2,1)}, bf16[1024,256]{1,0:T(8,128)(2,1)}, bf16[1024,256]{1,0:T(8,128)(2,1)}, bf16[1024,256]{1,0:T(8,128)(2,1)}) custom-call(s32[2]{0:T(128)S(1)} %pad_add_fusion.1.halves, bf16[1024,1024]{1,0:T(8,128)(2,1)S(1)} %copy-done.1), custom_call_target="tpu_custom_call" | custom-call | tf_op jit(solution)/shard_map/pallas_call | solution.py:192
  4.5 5.5 %collective-permute-start = (bf16[1024,256]{1,0:T(8,128)(2,1)}, bf16[1024,256]{1,0:T(8,128)(2,1)S(1)}, u32[]{:S(2)}, u32[]{:S(2)}) collective-permute-start(bf16[1024,256]{1,0:T(8,128)(2,1)} %get-tuple-element.17), channel_id=1, source_target_pairs={{0,0},{1,17},{2,2},{3,19},{4,4},{5,21},{6,6},{7,23},{8,8},{9,25},{... | collective-permute-start | bytes 1572872 | tf_op jit(solution)/shard_map/ppermute | solution.py:60
  10.0 0.5 collective-permute-start.1
  10.5 3.8 %collective-permute-start.2 = (bf16[1024,256]{1,0:T(8,128)(2,1)}, bf16[1024,256]{1,0:T(8,128)(2,1)S(1)}, u32[]{:S(2)}, u32[]{:S(2)}) collective-permute-start(bf16[1024,256]{1,0:T(8,128)(2,1)} %get-tuple-element.19), channel_id=1, source_target_pairs={{0,0},{1,17},{2,2},{3,19},{4,4},{5,21},{6,6},{7,23},{8,8},{9,25},{... | collective-permute-start | bytes 1572872 | tf_op jit(solution)/shard_map/ppermute | solution.py:60
  14.3 0.1 collective-permute-start.3
  14.4 0.6 dynamic_slice.3.count
  15.0 1.2 shard_map.51
  16.2 2.4 %copy-done = bf16[4,640,1024]{2,1,0:T(8,128)(2,1)} copy-done((bf16[4,640,1024]{2,1,0:T(8,128)(2,1)}, bf16[4,640,1024]{2,1,0:T(8,128)(2,1)S(1)}, u32[]{:S(2)}) %copy-start) | copy-done | bytes 5242904
  18.6 3.4 %collective-permute-done.near = bf16[1024,256]{1,0:T(8,128)(2,1)S(1)} collective-permute-done((bf16[1024,256]{1,0:T(8,128)(2,1)}, bf16[1024,256]{1,0:T(8,128)(2,1)S(1)}, u32[]{:S(2)}, u32[]{:S(2)}) %collective-permute-start) | collective-permute-done | bytes 524320 | tf_op jit(solution)/shard_map/ppermute | solution.py:60
  22.0 2.9 %collective-permute-done.1.far = bf16[1024,256]{1,0:T(8,128)(2,1)S(1)} collective-permute-done((bf16[1024,256]{1,0:T(8,128)(2,1)}, bf16[1024,256]{1,0:T(8,128)(2,1)S(1)}, u32[]{:S(2)}, u32[]{:S(2)}) %collective-permute-start.1) | collective-permute-done | bytes 524320 | tf_op jit(solution)/shard_map/ppermute | solution.py:60
  24.9 0.1 shard_map.52.refs_0_
  24.9 3.8 %collective-permute-start.7 = (bf16[2048,256]{1,0:T(8,128)(2,1)S(1)}, bf16[2048,256]{1,0:T(8,128)(2,1)}, u32[]{:S(2)}, u32[]{:S(2)}) collective-permute-start(bf16[2048,256]{1,0:T(8,128)(2,1)S(1)} %shard_map.52.refs_0_), channel_id=1, source_target_pairs={{0,2},{1,7},{2,4},{3,1},{4,6},{5,3},{6,0},{7,5},{8,10},{9,15},{10,... | collective-permute-start | bytes 3145736 | tf_op jit(solution)/shard_map/ppermute | solution.py:60
  28.8 4.1 %collective-permute-done.2.near = bf16[1024,256]{1,0:T(8,128)(2,1)S(1)} collective-permute-done((bf16[1024,256]{1,0:T(8,128)(2,1)}, bf16[1024,256]{1,0:T(8,128)(2,1)S(1)}, u32[]{:S(2)}, u32[]{:S(2)}) %collective-permute-start.2) | collective-permute-done | bytes 524320 | tf_op jit(solution)/shard_map/ppermute | solution.py:60
  32.8 1.5 collective-permute-done.3.far
  34.3 0.1 shard_map.53.refs_0_
  34.4 5.1 %all-to-all-start = ((bf16[4,640,1024]{2,1,0:T(8,128)(2,1)}), bf16[4,640,1024]{2,1,0:T(8,128)(2,1)}, u32[]{:S(2)}, u32[]{:S(2)}) async-start(bf16[4,640,1024]{2,1,0:T(8,128)(2,1)} %copy-done), calls=%async_computation | async-start | bytes 10485760 | tf_op jit(solution)/shard_map/all_to_all | solution.py:64
  39.5 3.8 %collective-permute-start.4 = (bf16[2048,256]{1,0:T(8,128)(2,1)S(1)}, bf16[2048,256]{1,0:T(8,128)(2,1)S(1)}, u32[]{:S(2)}, u32[]{:S(2)}) collective-permute-start(bf16[2048,256]{1,0:T(8,128)(2,1)S(1)} %shard_map.53.refs_0_), channel_id=1, source_target_pairs={{0,2},{1,7},{2,4},{3,1},{4,6},{5,3},{6,0},{7,5},{8,10},{9,15},{10,... | collective-permute-start | bytes 3145736 | tf_op jit(solution)/shard_map/ppermute | solution.py:60
  43.3 0.0 collective-permute-done.7.refs_1_
  43.3 0.9 collective-permute-start.8
  44.3 0.5 collective-permute-start.13
  44.8 10.3 %collective-permute-done.4.refs_1_ = bf16[2048,256]{1,0:T(8,128)(2,1)S(1)} collective-permute-done((bf16[2048,256]{1,0:T(8,128)(2,1)S(1)}, bf16[2048,256]{1,0:T(8,128)(2,1)S(1)}, u32[]{:S(2)}, u32[]{:S(2)}) %collective-permute-start.4) | collective-permute-done | bytes 1048608 | tf_op jit(solution)/shard_map/ppermute | solution.py:60
  55.1 0.0 collective-permute-done.5.refs_4_
  55.1 1.0 copy-done.5
  56.0 10.4 %collective-permute-done.8.refs_2_ = bf16[2048,256]{1,0:T(8,128)(2,1)S(1)} collective-permute-done((bf16[2048,256]{1,0:T(8,128)(2,1)}, bf16[2048,256]{1,0:T(8,128)(2,1)S(1)}, u32[]{:S(2)}, u32[]{:S(2)}) %collective-permute-start.8) | collective-permute-done | bytes 1048608 | tf_op jit(solution)/shard_map/ppermute | solution.py:60
  66.4 0.0 collective-permute-done.9.refs_5_
  66.4 1.0 copy-done.11
  67.4 3.4 %collective-permute-start.10 = (bf16[2048,256]{1,0:T(8,128)(2,1)S(1)}, bf16[2048,256]{1,0:T(8,128)(2,1)}, u32[]{:S(2)}, u32[]{:S(2)}) collective-permute-start(bf16[2048,256]{1,0:T(8,128)(2,1)S(1)} %collective-permute-done.8.refs_2_), channel_id=1, source_target_pairs={{0,2},{1,7},{2,4},{3,1},{4,6},{5,3},{6,0},{7,5},{8,10},{9,15},{10,... | collective-permute-start | bytes 3145736 | tf_op jit(solution)/shard_map/ppermute | solution.py:60
  70.8 0.0 collective-permute-start.6
  70.8 0.4 collective-permute-start.14
  71.3 0.1 collective-permute-start.11
  71.3 1.0 copy-done.7
  72.3 10.2 %collective-permute-done.10.refs_3_ = bf16[2048,256]{1,0:T(8,128)(2,1)} collective-permute-done((bf16[2048,256]{1,0:T(8,128)(2,1)S(1)}, bf16[2048,256]{1,0:T(8,128)(2,1)}, u32[]{:S(2)}, u32[]{:S(2)}) %collective-permute-start.10) | collective-permute-done | bytes 1048608 | tf_op jit(solution)/shard_map/ppermute | solution.py:60
  82.5 3.0 %collective-permute-start.12 = (bf16[2048,256]{1,0:T(8,128)(2,1)}, bf16[2048,256]{1,0:T(8,128)(2,1)}, u32[]{:S(2)}, u32[]{:S(2)}) collective-permute-start(bf16[2048,256]{1,0:T(8,128)(2,1)} %collective-permute-done.10.refs_3_), channel_id=1, source_target_pairs={{0,1},{1,0},{2,3},{3,2},{4,5},{5,4},{6,7},{7,6},{8,9},{9,8},{10,11... | collective-permute-start | bytes 3145736 | tf_op jit(solution)/shard_map/ppermute | solution.py:60
  85.6 0.0 collective-permute-done.13.refs_4_
  85.6 1.0 copy-done.3
  86.5 7.2 %collective-permute-done.6.refs_2_ = bf16[2048,256]{1,0:T(8,128)(2,1)} collective-permute-done((bf16[2048,256]{1,0:T(8,128)(2,1)S(1)}, bf16[2048,256]{1,0:T(8,128)(2,1)}, u32[]{:S(2)}, u32[]{:S(2)}) %collective-permute-start.6) | collective-permute-done | bytes 1048608 | tf_op jit(solution)/shard_map/ppermute | solution.py:60
  93.8 1.0 copy-done.9
  94.8 0.0 collective-permute-done.11.refs_6_
  94.8 1.0 copy-done.13
  95.8 3.5 %collective-permute-start.15 = (bf16[2048,256]{1,0:T(8,128)(2,1)}, bf16[2048,256]{1,0:T(8,128)(2,1)}, u32[]{:S(2)}, u32[]{:S(2)}) collective-permute-start(bf16[2048,256]{1,0:T(8,128)(2,1)} %collective-permute-done.6.refs_2_), channel_id=1, source_target_pairs={{0,2},{1,7},{2,4},{3,1},{4,6},{5,3},{6,0},{7,5},{8,10},{9,15},{10,... | collective-permute-start | bytes 3145736 | tf_op jit(solution)/shard_map/ppermute | solution.py:60
  99.3 0.1 pad_add_fusion.2
  99.4 0.0 collective-permute-start.16
  99.4 0.0 collective-permute-done.12.refs_7_
  99.5 1.2 copy-done.6
  100.7 1.2 copy-done.8
  101.9 1.2 copy-done.12
  103.1 1.2 copy-done.14
  104.4 11.8 %shard_map.54 = s16[4,2,672,128]{3,2,1,0:T(8,128)(2,1)} custom-call(s32[8]{0:T(128)S(1)} %get-tuple-element.39.table, bf16[4,640,1024]{2,1,0:T(8,128)(2,1)} %all-to-all-done.grads, bf16[2048,256]{1,0:T(8,128)(2,1)S(1)} %shard_map.52.refs_0_, bf16[2048,256]{1,0:T(8,128)(2,1)} %collective-permute-done.7.refs_1_, bf16[2048,256]{1,0:T(8,128)(2,1)S(1)} %copy-done.8, ...), custom_call_target="tpu_custom_call" | custom-call | tf_op jit(solution)/shard_map/pallas_call | solution.py:192
  116.2 1.1 collective-permute-start.17
  117.3 4.2 %all-to-all-start.1 = ((s16[4,2,672,128]{3,2,1,0:T(8,128)(2,1)}), s16[4,2,672,128]{3,2,1,0:T(8,128)(2,1)S(1)}, u32[]{:S(2)}, u32[]{:S(2)}) async-start(s16[4,2,672,128]{3,2,1,0:T(8,128)(2,1)} %shard_map.54), calls=%async_computation.1 | async-start | bytes 2752512 | tf_op jit(solution)/shard_map/all_to_all | solution.py:64
  121.5 1.2 copy-done.4
  122.7 1.2 copy-done.10
  123.9 9.7 %shard_map.55 = s16[4,2,672,128]{3,2,1,0:T(8,128)(2,1)S(1)} custom-call(s32[8]{0:T(128)S(1)} %get-tuple-element.38.table, bf16[4,640,1024]{2,1,0:T(8,128)(2,1)} %all-to-all-done.grads, bf16[2048,256]{1,0:T(8,128)(2,1)S(1)} %shard_map.53.refs_0_, bf16[2048,256]{1,0:T(8,128)(2,1)S(1)} %collective-permute-done.4.refs_1_, ...), custom_call_target="tpu_custom_call" | custom-call | tf_op jit(solution)/shard_map/pallas_call | solution.py:192
  133.7 0.8 slice_bitcast_fusion
  134.5 1.5 collective-permute-start.18
  135.9 2.4 %collective-permute-start.19 = (s16[2,672,128]{2,1,0:T(8,128)(2,1)S(1)}, s16[2,672,128]{2,1,0:T(8,128)(2,1)S(1)}, u32[]{:S(2)}, u32[]{:S(2)}) collective-permute-start(s16[2,672,128]{2,1,0:T(8,128)(2,1)S(1)} %get-tuple-element.35), channel_id=1, source_target_pairs={{0,64},{1,65},{2,66},{3,67},{4,68},{5,69},{6,70},{7,71},{8,72},{9,... | collective-permute-start | bytes 1032200 | tf_op jit(solution)/shard_map/ppermute | solution.py:60
  138.3 1.2 collective-permute-start.20
  139.5 0.4 all-to-all-done.1.refs_0_
  139.9 8.7 %collective-permute-done.18.refs_2_ = s16[2,672,128]{2,1,0:T(8,128)(2,1)S(1)} collective-permute-done((s16[2,672,128]{2,1,0:T(8,128)(2,1)}, s16[2,672,128]{2,1,0:T(8,128)(2,1)S(1)}, u32[]{:S(2)}, u32[]{:S(2)}) %collective-permute-start.18) | collective-permute-done | bytes 344096 | tf_op jit(solution)/shard_map/ppermute | solution.py:60
  148.6 6.1 %collective-permute-done.19.refs_3_ = s16[2,672,128]{2,1,0:T(8,128)(2,1)S(1)} collective-permute-done((s16[2,672,128]{2,1,0:T(8,128)(2,1)S(1)}, s16[2,672,128]{2,1,0:T(8,128)(2,1)S(1)}, u32[]{:S(2)}, u32[]{:S(2)}) %collective-permute-start.19) | collective-permute-done | bytes 344096 | tf_op jit(solution)/shard_map/ppermute | solution.py:60
  154.7 1.8 %shard_map.56 = (f32[512,640]{1,0:T(8,128)}, f32[16,128]{1,0:T(8,128)S(1)}) custom-call(s16[4,2,672,128]{3,2,1,0:T(8,128)(2,1)S(1)} %all-to-all-done.1.refs_0_, s16[2,672,128]{2,1,0:T(8,128)(2,1)S(1)} %get-tuple-element.37.refs_1_, s16[2,672,128]{2,1,0:T(8,128)(2,1)S(1)} %collective-permute-done.18.refs_2_, ...), custom_call_target="tpu_custom_call" | custom-call | tf_op jit(solution)/shard_map/pallas_call | solution.py:192
  156.4 0.6 slice_bitcast_fusion.4
  (27 shorter events, 0.1 us)
Async XLA Ops:
  0.6 13.8 %copy-start.15 = (s32[16]{0:T(128)S(1)}, s32[16]{0:T(128)}, u32[]{:S(2)}) copy-start(s32[16]{0:T(128)} %param.5) | copy-start | bytes 196
  0.7 1.6 %copy-start.1 = (bf16[1024,1024]{1,0:T(8,128)(2,1)S(1)}, bf16[1024,1024]{1,0:T(8,128)(2,1)}, u32[]{:S(2)}) copy-start(bf16[1024,1024]{1,0:T(8,128)(2,1)} %activations.1) | copy-start | bytes 6291460
  2.3 12.6 %copy-start.2 = (bf16[1024,640]{1,0:T(8,128)(2,1)S(1)}, bf16[1024,640]{1,0:T(8,128)(2,1)}, u32[]{:S(2)}) copy-start(bf16[1024,640]{1,0:T(8,128)(2,1)} %out_grad) | copy-start | bytes 3932164
  4.5 17.5 %collective-permute-start = (bf16[1024,256]{1,0:T(8,128)(2,1)}, bf16[1024,256]{1,0:T(8,128)(2,1)S(1)}, u32[]{:S(2)}, u32[]{:S(2)}) collective-permute-start(bf16[1024,256]{1,0:T(8,128)(2,1)} %get-tuple-element.17), channel_id=1, source_target_pairs={{0,0},{1,17},{2,2},{3,19},{4,4},{5,21},{6,6},{7,23},{8,8},{9,25},{... | collective-permute-start | bytes 1572872 | tf_op jit(solution)/shard_map/ppermute | solution.py:60
  10.0 14.9 %collective-permute-start.1 = (bf16[1024,256]{1,0:T(8,128)(2,1)}, bf16[1024,256]{1,0:T(8,128)(2,1)S(1)}, u32[]{:S(2)}, u32[]{:S(2)}) collective-permute-start(bf16[1024,256]{1,0:T(8,128)(2,1)} %get-tuple-element.18), channel_id=1, source_target_pairs={{0,8},{1,25},{2,10},{3,27},{4,12},{5,29},{6,14},{7,31},{8,1},{9,16... | collective-permute-start | bytes 1572872 | tf_op jit(solution)/shard_map/ppermute | solution.py:60
  10.5 22.4 %collective-permute-start.2 = (bf16[1024,256]{1,0:T(8,128)(2,1)}, bf16[1024,256]{1,0:T(8,128)(2,1)S(1)}, u32[]{:S(2)}, u32[]{:S(2)}) collective-permute-start(bf16[1024,256]{1,0:T(8,128)(2,1)} %get-tuple-element.19), channel_id=1, source_target_pairs={{0,0},{1,17},{2,2},{3,19},{4,4},{5,21},{6,6},{7,23},{8,8},{9,25},{... | collective-permute-start | bytes 1572872 | tf_op jit(solution)/shard_map/ppermute | solution.py:60
  14.3 20.0 %collective-permute-start.3 = (bf16[1024,256]{1,0:T(8,128)(2,1)}, bf16[1024,256]{1,0:T(8,128)(2,1)S(1)}, u32[]{:S(2)}, u32[]{:S(2)}) collective-permute-start(bf16[1024,256]{1,0:T(8,128)(2,1)} %get-tuple-element.20), channel_id=1, source_target_pairs={{0,8},{1,25},{2,10},{3,27},{4,12},{5,29},{6,14},{7,31},{8,1},{9,16... | collective-permute-start | bytes 1572872 | tf_op jit(solution)/shard_map/ppermute | solution.py:60
  16.2 2.4 %copy-start = (bf16[4,640,1024]{2,1,0:T(8,128)(2,1)}, bf16[4,640,1024]{2,1,0:T(8,128)(2,1)S(1)}, u32[]{:S(2)}) copy-start(bf16[4,640,1024]{2,1,0:T(8,128)(2,1)S(1)} %shard_map.51) | copy-start | bytes 15728644
  24.9 18.4 %collective-permute-start.7 = (bf16[2048,256]{1,0:T(8,128)(2,1)S(1)}, bf16[2048,256]{1,0:T(8,128)(2,1)}, u32[]{:S(2)}, u32[]{:S(2)}) collective-permute-start(bf16[2048,256]{1,0:T(8,128)(2,1)S(1)} %shard_map.52.refs_0_), channel_id=1, source_target_pairs={{0,2},{1,7},{2,4},{3,1},{4,6},{5,3},{6,0},{7,5},{8,10},{9,15},{10,... | collective-permute-start | bytes 3145736 | tf_op jit(solution)/shard_map/ppermute | solution.py:60
  34.4 65.1 %all-to-all-start = ((bf16[4,640,1024]{2,1,0:T(8,128)(2,1)}), bf16[4,640,1024]{2,1,0:T(8,128)(2,1)}, u32[]{:S(2)}, u32[]{:S(2)}) async-start(bf16[4,640,1024]{2,1,0:T(8,128)(2,1)} %copy-done), calls=%async_computation | async-start | bytes 10485760 | tf_op jit(solution)/shard_map/all_to_all | solution.py:64
  39.5 15.6 %collective-permute-start.4 = (bf16[2048,256]{1,0:T(8,128)(2,1)S(1)}, bf16[2048,256]{1,0:T(8,128)(2,1)S(1)}, u32[]{:S(2)}, u32[]{:S(2)}) collective-permute-start(bf16[2048,256]{1,0:T(8,128)(2,1)S(1)} %shard_map.53.refs_0_), channel_id=1, source_target_pairs={{0,2},{1,7},{2,4},{3,1},{4,6},{5,3},{6,0},{7,5},{8,10},{9,15},{10,... | collective-permute-start | bytes 3145736 | tf_op jit(solution)/shard_map/ppermute | solution.py:60
  43.3 11.7 %collective-permute-start.5 = (bf16[2048,256]{1,0:T(8,128)(2,1)S(1)}, bf16[2048,256]{1,0:T(8,128)(2,1)S(1)}, u32[]{:S(2)}, u32[]{:S(2)}) collective-permute-start(bf16[2048,256]{1,0:T(8,128)(2,1)S(1)} %shard_map.52.refs_0_), channel_id=1, source_target_pairs={{0,1},{1,0},{2,3},{3,2},{4,5},{5,4},{6,7},{7,6},{8,9},{9,8},{10,11... | collective-permute-start | bytes 3145736 | tf_op jit(solution)/shard_map/ppermute | solution.py:60
  43.3 23.1 %collective-permute-start.8 = (bf16[2048,256]{1,0:T(8,128)(2,1)}, bf16[2048,256]{1,0:T(8,128)(2,1)S(1)}, u32[]{:S(2)}, u32[]{:S(2)}) collective-permute-start(bf16[2048,256]{1,0:T(8,128)(2,1)} %collective-permute-done.7.refs_1_), channel_id=1, source_target_pairs={{0,2},{1,7},{2,4},{3,1},{4,6},{5,3},{6,0},{7,5},{8,10},{9,15},{10,... | collective-permute-start | bytes 3145736 | tf_op jit(solution)/shard_map/ppermute | solution.py:60
  44.3 22.1 %collective-permute-start.9 = (bf16[2048,256]{1,0:T(8,128)(2,1)}, bf16[2048,256]{1,0:T(8,128)(2,1)S(1)}, u32[]{:S(2)}, u32[]{:S(2)}) collective-permute-start(bf16[2048,256]{1,0:T(8,128)(2,1)} %collective-permute-done.7.refs_1_), channel_id=1, source_target_pairs={{0,1},{1,0},{2,3},{3,2},{4,5},{5,4},{6,7},{7,6},{8,9},{9,8},{10,11... | collective-permute-start | bytes 3145736 | tf_op jit(solution)/shard_map/ppermute | solution.py:60
  44.3 41.3 %collective-permute-start.13 = (bf16[2048,256]{1,0:T(8,128)(2,1)S(1)}, bf16[2048,256]{1,0:T(8,128)(2,1)S(1)}, u32[]{:S(2)}, u32[]{:S(2)}) collective-permute-start(bf16[2048,256]{1,0:T(8,128)(2,1)S(1)} %shard_map.53.refs_0_), channel_id=1, source_target_pairs={{0,1},{1,0},{2,3},{3,2},{4,5},{5,4},{6,7},{7,6},{8,9},{9,8},{10,11... | collective-permute-start | bytes 3145736 | tf_op jit(solution)/shard_map/ppermute | solution.py:60
  55.1 1.0 copy-start.5
  66.4 1.0 copy-start.11
  67.4 15.2 %collective-permute-start.10 = (bf16[2048,256]{1,0:T(8,128)(2,1)S(1)}, bf16[2048,256]{1,0:T(8,128)(2,1)}, u32[]{:S(2)}, u32[]{:S(2)}) collective-permute-start(bf16[2048,256]{1,0:T(8,128)(2,1)S(1)} %collective-permute-done.8.refs_2_), channel_id=1, source_target_pairs={{0,2},{1,7},{2,4},{3,1},{4,6},{5,3},{6,0},{7,5},{8,10},{9,15},{10,... | collective-permute-start | bytes 3145736 | tf_op jit(solution)/shard_map/ppermute | solution.py:60
  70.8 23.0 %collective-permute-start.6 = (bf16[2048,256]{1,0:T(8,128)(2,1)S(1)}, bf16[2048,256]{1,0:T(8,128)(2,1)}, u32[]{:S(2)}, u32[]{:S(2)}) collective-permute-start(bf16[2048,256]{1,0:T(8,128)(2,1)S(1)} %collective-permute-done.4.refs_1_), channel_id=1, source_target_pairs={{0,2},{1,7},{2,4},{3,1},{4,6},{5,3},{6,0},{7,5},{8,10},{9,15},{10,... | collective-permute-start | bytes 3145736 | tf_op jit(solution)/shard_map/ppermute | solution.py:60
  70.8 22.9 %collective-permute-start.14 = (bf16[2048,256]{1,0:T(8,128)(2,1)S(1)}, bf16[2048,256]{1,0:T(8,128)(2,1)S(1)}, u32[]{:S(2)}, u32[]{:S(2)}) collective-permute-start(bf16[2048,256]{1,0:T(8,128)(2,1)S(1)} %collective-permute-done.4.refs_1_), channel_id=1, source_target_pairs={{0,1},{1,0},{2,3},{3,2},{4,5},{5,4},{6,7},{7,6},{8,9},{9,8},{10,11... | collective-permute-start | bytes 3145736 | tf_op jit(solution)/shard_map/ppermute | solution.py:60
  71.3 23.5 %collective-permute-start.11 = (bf16[2048,256]{1,0:T(8,128)(2,1)S(1)}, bf16[2048,256]{1,0:T(8,128)(2,1)S(1)}, u32[]{:S(2)}, u32[]{:S(2)}) collective-permute-start(bf16[2048,256]{1,0:T(8,128)(2,1)S(1)} %collective-permute-done.8.refs_2_), channel_id=1, source_target_pairs={{0,1},{1,0},{2,3},{3,2},{4,5},{5,4},{6,7},{7,6},{8,9},{9,8},{10,11... | collective-permute-start | bytes 3145736 | tf_op jit(solution)/shard_map/ppermute | solution.py:60
  71.3 1.0 copy-start.7
  82.5 16.9 %collective-permute-start.12 = (bf16[2048,256]{1,0:T(8,128)(2,1)}, bf16[2048,256]{1,0:T(8,128)(2,1)}, u32[]{:S(2)}, u32[]{:S(2)}) collective-permute-start(bf16[2048,256]{1,0:T(8,128)(2,1)} %collective-permute-done.10.refs_3_), channel_id=1, source_target_pairs={{0,1},{1,0},{2,3},{3,2},{4,5},{5,4},{6,7},{7,6},{8,9},{9,8},{10,11... | collective-permute-start | bytes 3145736 | tf_op jit(solution)/shard_map/ppermute | solution.py:60
  85.6 1.0 copy-start.3
  93.8 1.0 copy-start.9
  94.8 1.0 copy-start.13
  95.8 20.4 %collective-permute-start.15 = (bf16[2048,256]{1,0:T(8,128)(2,1)}, bf16[2048,256]{1,0:T(8,128)(2,1)}, u32[]{:S(2)}, u32[]{:S(2)}) collective-permute-start(bf16[2048,256]{1,0:T(8,128)(2,1)} %collective-permute-done.6.refs_2_), channel_id=1, source_target_pairs={{0,2},{1,7},{2,4},{3,1},{4,6},{5,3},{6,0},{7,5},{8,10},{9,15},{10,... | collective-permute-start | bytes 3145736 | tf_op jit(solution)/shard_map/ppermute | solution.py:60
  99.4 22.1 %collective-permute-start.16 = (bf16[2048,256]{1,0:T(8,128)(2,1)}, bf16[2048,256]{1,0:T(8,128)(2,1)}, u32[]{:S(2)}, u32[]{:S(2)}) collective-permute-start(bf16[2048,256]{1,0:T(8,128)(2,1)} %collective-permute-done.6.refs_2_), channel_id=1, source_target_pairs={{0,1},{1,0},{2,3},{3,2},{4,5},{5,4},{6,7},{7,6},{8,9},{9,8},{10,11... | collective-permute-start | bytes 3145736 | tf_op jit(solution)/shard_map/ppermute | solution.py:60
  99.5 1.2 copy-start.6
  100.7 1.2 copy-start.8
  101.9 1.2 copy-start.12
  103.1 1.2 copy-start.14
  116.2 5.3 %collective-permute-start.17 = (bf16[2048,256]{1,0:T(8,128)(2,1)}, bf16[2048,256]{1,0:T(8,128)(2,1)}, u32[]{:S(2)}, u32[]{:S(2)}) collective-permute-start(bf16[2048,256]{1,0:T(8,128)(2,1)} %collective-permute-done.15.refs_3_), channel_id=1, source_target_pairs={{0,1},{1,0},{2,3},{3,2},{4,5},{5,4},{6,7},{7,6},{8,9},{9,8},{10,11... | collective-permute-start | bytes 3145736 | tf_op jit(solution)/shard_map/ppermute | solution.py:60
  117.3 22.6 %all-to-all-start.1 = ((s16[4,2,672,128]{3,2,1,0:T(8,128)(2,1)}), s16[4,2,672,128]{3,2,1,0:T(8,128)(2,1)S(1)}, u32[]{:S(2)}, u32[]{:S(2)}) async-start(s16[4,2,672,128]{3,2,1,0:T(8,128)(2,1)} %shard_map.54), calls=%async_computation.1 | async-start | bytes 2752512 | tf_op jit(solution)/shard_map/all_to_all | solution.py:64
  121.5 1.2 copy-start.4
  122.7 1.2 copy-start.10
  134.5 14.1 %collective-permute-start.18 = (s16[2,672,128]{2,1,0:T(8,128)(2,1)}, s16[2,672,128]{2,1,0:T(8,128)(2,1)S(1)}, u32[]{:S(2)}, u32[]{:S(2)}) collective-permute-start(s16[2,672,128]{2,1,0:T(8,128)(2,1)} %get-tuple-element.36), channel_id=1, source_target_pairs={{0,32},{1,33},{2,34},{3,35},{4,36},{5,37},{6,38},{7,39},{8,40},{9,... | collective-permute-start | bytes 1032200 | tf_op jit(solution)/shard_map/ppermute | solution.py:60
  135.9 18.7 %collective-permute-start.19 = (s16[2,672,128]{2,1,0:T(8,128)(2,1)S(1)}, s16[2,672,128]{2,1,0:T(8,128)(2,1)S(1)}, u32[]{:S(2)}, u32[]{:S(2)}) collective-permute-start(s16[2,672,128]{2,1,0:T(8,128)(2,1)S(1)} %get-tuple-element.35), channel_id=1, source_target_pairs={{0,64},{1,65},{2,66},{3,67},{4,68},{5,69},{6,70},{7,71},{8,72},{9,... | collective-permute-start | bytes 1032200 | tf_op jit(solution)/shard_map/ppermute | solution.py:60
  138.3 16.3 %collective-permute-start.20 = (s16[2,672,128]{2,1,0:T(8,128)(2,1)S(1)}, s16[2,672,128]{2,1,0:T(8,128)(2,1)S(1)}, u32[]{:S(2)}, u32[]{:S(2)}) collective-permute-start(s16[2,672,128]{2,1,0:T(8,128)(2,1)S(1)} %get-tuple-element.34), channel_id=1, source_target_pairs={{0,96},{1,97},{2,98},{3,99},{4,100},{5,101},{6,102},{7,103},{8,104... | collective-permute-start | bytes 1032200 | tf_op jit(solution)/shard_map/ppermute | solution.py:60

commit v4 on v3

--- a/solution.py
+++ b/solution.py
@@ -163,12 +163,12 @@
 
 def reduce(counts, *refs):
     messages, (out, bias_out) = refs[:-2], refs[-2:]
-    rows = messages[0].shape[-2] - EXTRA
+    rows = out.shape[1]
     at = 0
     for count in counts:
         mine, messages = messages[:count], messages[count:]
         sources = [(m, ()) for m in mine] if count > 1 else [(mine[0], (n,)) for n in range(SIDE)]
-        if at == 0:
+        if mine[0].shape[-2] == rows + EXTRA:
             bias_out[...] = sum(unpack_bias(m, (*n, 0), rows) for m, n in sources)
         for part in range(mine[0].shape[-3]):
             total = sum(unpack(m, (*n, part), rows) for m, n in sources)
@@ -221,7 +221,7 @@
     def sums(table, grads, held, other, with_bias):
         (message,) = kernel(
             functools.partial(multiply, with_bias),
-            [shape(jnp.int16, SIDE, parts, width + EXTRA, LANES)],
+            [shape(jnp.int16, SIDE, parts, width + (EXTRA if with_bias else TILE), LANES)],
             table,
             grads,
             *held,
@@ -249,9 +249,9 @@
     ring[1].append(send(after(ring[1][2], *other[1], other[0][2]), RING_Z))
     other[1].append(send(ring[1][2], SWAP))
     other[0].append(send(ring[0][3], SWAP))
-    early = sums(tables[0], grads, [after(ring[0][0], ring[1][2]), *ring[0][1:]], other[0], True)
+    early = sums(tables[0], grads, [after(ring[0][0], ring[1][2]), *ring[0][1:]], other[0], False)
     other[1].append(send(after(ring[1][3], early), SWAP))
-    late = sums(tables[1], grads, ring[1], other[1], False)
+    late = sums(tables[1], grads, ring[1], other[1], True)
     messages = [
         [swap_all(after(early, ring[1][3]), ALONG_Y)],
         [late[0]] + [send(late[d], AWAY_Y[d]) for d in range(1, SIDE)],

time: 158 us -> 157 us (level)
  transfers between devices with their start and end apart: 23 -> 23, of which waited for: 11 -> 10; matrix products, arithmetic and copies ran while one was open for 1% -> 1% of each run, Pallas kernels for 15% -> 15%
where the time goes in v4:
time: 157 us; the launch traced here: 156 us
  waiting for transfers between devices  64 us (41%)
  starting transfers between devices  44.8 us (29%)
  Pallas kernels  26.9 us (17%)
  local copies, waits for them, and re-layouts  19.2 us (12%)
    ppermute x21, waiting for transfers between devices, send(): return lax.ppermute(value, AXES, perm)  64 us
    ppermute x21, starting transfers between devices, send(): return lax.ppermute(value, AXES, perm)  35.6 us
    pallas_call x7, Pallas kernels, kernel(): pl.pallas_call(body, out_shape=out_shape, in_specs=[scalars()] * (scalar...  26.9 us
    unnamed x32, local copies, waits for them, and re-layouts  17.2 us
    all_to_all x2, starting transfers between devices, swap_all(): lax.all_to_all(value, AXES, 0, 0, axis_index_groups=groups, tiled=True)  9.28 us
  transfers between devices with their start and end apart: 23, of which 10 were waited for; matrix products, arithmetic and copies ran while one was open for 1% of the time, Pallas kernels for 15%

profile of v4, /device:TPU:1, one launch (start us, length us, event | category | flops | bytes accessed | tf_op | source)
XLA Modules:
  0.0 155.9 jit_solution(17806001203102578116)
XLA Ops:
  0.7 0.1 pad_add_fusion.1.halves
  0.7 1.6 %copy-done.1 = bf16[1024,1024]{1,0:T(8,128)(2,1)S(1)} copy-done((bf16[1024,1024]{1,0:T(8,128)(2,1)S(1)}, bf16[1024,1024]{1,0:T(8,128)(2,1)}, u32[]{:S(2)}) %copy-start.1) | copy-done | bytes 2097176
  2.3 2.2 %shard_map.50 = (bf16[1024,256]{1,0:T(8,128)(2,1)}, bf16[1024,256]{1,0:T(8,128)(2,1)}, bf16[1024,256]{1,0:T(8,128)(2,1)}, bf16[1024,256]{1,0:T(8,128)(2,1)}) custom-call(s32[2]{0:T(128)S(1)} %pad_add_fusion.1.halves, bf16[1024,1024]{1,0:T(8,128)(2,1)S(1)} %copy-done.1), custom_call_target="tpu_custom_call" | custom-call | tf_op jit(solution)/shard_map/pallas_call | solution.py:192
  4.5 5.5 %collective-permute-start = (bf16[1024,256]{1,0:T(8,128)(2,1)}, bf16[1024,256]{1,0:T(8,128)(2,1)S(1)}, u32[]{:S(2)}, u32[]{:S(2)}) collective-permute-start(bf16[1024,256]{1,0:T(8,128)(2,1)} %get-tuple-element.17), channel_id=1, source_target_pairs={{0,0},{1,17},{2,2},{3,19},{4,4},{5,21},{6,6},{7,23},{8,8},{9,25},{... | collective-permute-start | bytes 1572872 | tf_op jit(solution)/shard_map/ppermute | solution.py:60
  10.0 0.5 collective-permute-start.1
  10.5 3.8 %collective-permute-start.2 = (bf16[1024,256]{1,0:T(8,128)(2,1)}, bf16[1024,256]{1,0:T(8,128)(2,1)S(1)}, u32[]{:S(2)}, u32[]{:S(2)}) collective-permute-start(bf16[1024,256]{1,0:T(8,128)(2,1)} %get-tuple-element.19), channel_id=1, source_target_pairs={{0,0},{1,17},{2,2},{3,19},{4,4},{5,21},{6,6},{7,23},{8,8},{9,25},{... | collective-permute-start | bytes 1572872 | tf_op jit(solution)/shard_map/ppermute | solution.py:60
  14.3 0.1 collective-permute-start.3
  14.4 0.6 dynamic_slice.3.count
  15.0 1.2 shard_map.51
  16.2 2.4 %copy-done = bf16[4,640,1024]{2,1,0:T(8,128)(2,1)} copy-done((bf16[4,640,1024]{2,1,0:T(8,128)(2,1)}, bf16[4,640,1024]{2,1,0:T(8,128)(2,1)S(1)}, u32[]{:S(2)}) %copy-start) | copy-done | bytes 5242904
  18.6 3.4 %collective-permute-done.near = bf16[1024,256]{1,0:T(8,128)(2,1)S(1)} collective-permute-done((bf16[1024,256]{1,0:T(8,128)(2,1)}, bf16[1024,256]{1,0:T(8,128)(2,1)S(1)}, u32[]{:S(2)}, u32[]{:S(2)}) %collective-permute-start) | collective-permute-done | bytes 524320 | tf_op jit(solution)/shard_map/ppermute | solution.py:60
  22.0 2.9 %collective-permute-done.1.far = bf16[1024,256]{1,0:T(8,128)(2,1)S(1)} collective-permute-done((bf16[1024,256]{1,0:T(8,128)(2,1)}, bf16[1024,256]{1,0:T(8,128)(2,1)S(1)}, u32[]{:S(2)}, u32[]{:S(2)}) %collective-permute-start.1) | collective-permute-done | bytes 524320 | tf_op jit(solution)/shard_map/ppermute | solution.py:60
  24.9 0.1 shard_map.52.refs_0_
  24.9 3.8 %collective-permute-start.7 = (bf16[2048,256]{1,0:T(8,128)(2,1)S(1)}, bf16[2048,256]{1,0:T(8,128)(2,1)}, u32[]{:S(2)}, u32[]{:S(2)}) collective-permute-start(bf16[2048,256]{1,0:T(8,128)(2,1)S(1)} %shard_map.52.refs_0_), channel_id=1, source_target_pairs={{0,2},{1,7},{2,4},{3,1},{4,6},{5,3},{6,0},{7,5},{8,10},{9,15},{10,... | collective-permute-start | bytes 3145736 | tf_op jit(solution)/shard_map/ppermute | solution.py:60
  28.8 4.1 %collective-permute-done.2.near = bf16[1024,256]{1,0:T(8,128)(2,1)S(1)} collective-permute-done((bf16[1024,256]{1,0:T(8,128)(2,1)}, bf16[1024,256]{1,0:T(8,128)(2,1)S(1)}, u32[]{:S(2)}, u32[]{:S(2)}) %collective-permute-start.2) | collective-permute-done | bytes 524320 | tf_op jit(solution)/shard_map/ppermute | solution.py:60
  32.8 1.5 collective-permute-done.3.far
  34.3 0.1 shard_map.53.refs_0_
  34.4 5.1 %all-to-all-start = ((bf16[4,640,1024]{2,1,0:T(8,128)(2,1)}), bf16[4,640,1024]{2,1,0:T(8,128)(2,1)}, u32[]{:S(2)}, u32[]{:S(2)}) async-start(bf16[4,640,1024]{2,1,0:T(8,128)(2,1)} %copy-done), calls=%async_computation | async-start | bytes 10485760 | tf_op jit(solution)/shard_map/all_to_all | solution.py:64
  39.5 3.8 %collective-permute-start.4 = (bf16[2048,256]{1,0:T(8,128)(2,1)S(1)}, bf16[2048,256]{1,0:T(8,128)(2,1)S(1)}, u32[]{:S(2)}, u32[]{:S(2)}) collective-permute-start(bf16[2048,256]{1,0:T(8,128)(2,1)S(1)} %shard_map.53.refs_0_), channel_id=1, source_target_pairs={{0,2},{1,7},{2,4},{3,1},{4,6},{5,3},{6,0},{7,5},{8,10},{9,15},{10,... | collective-permute-start | bytes 3145736 | tf_op jit(solution)/shard_map/ppermute | solution.py:60
  43.3 0.9 collective-permute-start.8
  44.3 0.0 collective-permute-start.9
  44.3 0.5 collective-permute-start.13
  44.8 10.3 %collective-permute-done.4.refs_1_ = bf16[2048,256]{1,0:T(8,128)(2,1)S(1)} collective-permute-done((bf16[2048,256]{1,0:T(8,128)(2,1)S(1)}, bf16[2048,256]{1,0:T(8,128)(2,1)S(1)}, u32[]{:S(2)}, u32[]{:S(2)}) %collective-permute-start.4) | collective-permute-done | bytes 1048608 | tf_op jit(solution)/shard_map/ppermute | solution.py:60
  55.1 0.0 collective-permute-done.5.refs_4_
  55.1 1.0 copy-done.5
  56.0 10.4 %collective-permute-done.8.refs_2_ = bf16[2048,256]{1,0:T(8,128)(2,1)S(1)} collective-permute-done((bf16[2048,256]{1,0:T(8,128)(2,1)}, bf16[2048,256]{1,0:T(8,128)(2,1)S(1)}, u32[]{:S(2)}, u32[]{:S(2)}) %collective-permute-start.8) | collective-permute-done | bytes 1048608 | tf_op jit(solution)/shard_map/ppermute | solution.py:60
  66.4 1.0 copy-done.11
  67.4 3.4 %collective-permute-start.10 = (bf16[2048,256]{1,0:T(8,128)(2,1)S(1)}, bf16[2048,256]{1,0:T(8,128)(2,1)}, u32[]{:S(2)}, u32[]{:S(2)}) collective-permute-start(bf16[2048,256]{1,0:T(8,128)(2,1)S(1)} %collective-permute-done.8.refs_2_), channel_id=1, source_target_pairs={{0,2},{1,7},{2,4},{3,1},{4,6},{5,3},{6,0},{7,5},{8,10},{9,15},{10,... | collective-permute-start | bytes 3145736 | tf_op jit(solution)/shard_map/ppermute | solution.py:60
  70.8 0.0 collective-permute-start.6
  70.8 0.4 collective-permute-start.14
  71.3 0.1 collective-permute-start.11
  71.3 1.0 copy-done.7
  72.3 10.2 %collective-permute-done.10.refs_3_ = bf16[2048,256]{1,0:T(8,128)(2,1)} collective-permute-done((bf16[2048,256]{1,0:T(8,128)(2,1)S(1)}, bf16[2048,256]{1,0:T(8,128)(2,1)}, u32[]{:S(2)}, u32[]{:S(2)}) %collective-permute-start.10) | collective-permute-done | bytes 1048608 | tf_op jit(solution)/shard_map/ppermute | solution.py:60
  82.5 3.0 %collective-permute-start.12 = (bf16[2048,256]{1,0:T(8,128)(2,1)}, bf16[2048,256]{1,0:T(8,128)(2,1)}, u32[]{:S(2)}, u32[]{:S(2)}) collective-permute-start(bf16[2048,256]{1,0:T(8,128)(2,1)} %collective-permute-done.10.refs_3_), channel_id=1, source_target_pairs={{0,1},{1,0},{2,3},{3,2},{4,5},{5,4},{6,7},{7,6},{8,9},{9,8},{10,11... | collective-permute-start | bytes 3145736 | tf_op jit(solution)/shard_map/ppermute | solution.py:60
  85.6 1.0 copy-done.3
  86.5 7.2 %collective-permute-done.6.refs_2_ = bf16[2048,256]{1,0:T(8,128)(2,1)} collective-permute-done((bf16[2048,256]{1,0:T(8,128)(2,1)S(1)}, bf16[2048,256]{1,0:T(8,128)(2,1)}, u32[]{:S(2)}, u32[]{:S(2)}) %collective-permute-start.6) | collective-permute-done | bytes 1048608 | tf_op jit(solution)/shard_map/ppermute | solution.py:60
  93.8 0.0 collective-permute-done.14.refs_5_
  93.8 1.0 copy-done.9
  94.8 0.0 collective-permute-done.11.refs_6_
  94.8 1.0 copy-done.13
  95.8 3.5 %collective-permute-start.15 = (bf16[2048,256]{1,0:T(8,128)(2,1)}, bf16[2048,256]{1,0:T(8,128)(2,1)}, u32[]{:S(2)}, u32[]{:S(2)}) collective-permute-start(bf16[2048,256]{1,0:T(8,128)(2,1)} %collective-permute-done.6.refs_2_), channel_id=1, source_target_pairs={{0,2},{1,7},{2,4},{3,1},{4,6},{5,3},{6,0},{7,5},{8,10},{9,15},{10,... | collective-permute-start | bytes 3145736 | tf_op jit(solution)/shard_map/ppermute | solution.py:60
  99.3 0.1 pad_add_fusion.2
  99.4 0.0 collective-permute-start.16
  99.4 0.0 all-to-all-done.grads
  99.4 0.0 collective-permute-done.12.refs_7_
  99.5 1.2 copy-done.6
  100.7 1.2 copy-done.8
  101.9 1.2 copy-done.12
  103.1 1.2 copy-done.14
  104.4 10.6 %shard_map.54 = s16[4,2,656,128]{3,2,1,0:T(8,128)(2,1)} custom-call(s32[8]{0:T(128)S(1)} %get-tuple-element.39.table, bf16[4,640,1024]{2,1,0:T(8,128)(2,1)} %all-to-all-done.grads, bf16[2048,256]{1,0:T(8,128)(2,1)S(1)} %shard_map.52.refs_0_, bf16[2048,256]{1,0:T(8,128)(2,1)} %collective-permute-done.7.refs_1_, bf16[2048,256]{1,0:T(8,128)(2,1)S(1)} %copy-done.8, ...), custom_call_target="tpu_custom_call" | custom-call | tf_op jit(solution)/shard_map/pallas_call | solution.py:192
  115.0 0.0 collective-permute-done.15.refs_3_
  115.0 1.1 collective-permute-start.17
  116.0 4.2 %all-to-all-start.1 = ((s16[4,2,656,128]{3,2,1,0:T(8,128)(2,1)}), s16[4,2,656,128]{3,2,1,0:T(8,128)(2,1)S(1)}, u32[]{:S(2)}, u32[]{:S(2)}) async-start(s16[4,2,656,128]{3,2,1,0:T(8,128)(2,1)} %shard_map.54), calls=%async_computation.1 | async-start | bytes 2686976 | tf_op jit(solution)/shard_map/all_to_all | solution.py:64
  120.2 1.2 copy-done.4
  121.5 1.2 copy-done.10
  122.7 11.0 %shard_map.55 = s16[4,2,672,128]{3,2,1,0:T(8,128)(2,1)S(1)} custom-call(s32[8]{0:T(128)S(1)} %get-tuple-element.38.table, bf16[4,640,1024]{2,1,0:T(8,128)(2,1)} %all-to-all-done.grads, bf16[2048,256]{1,0:T(8,128)(2,1)S(1)} %shard_map.53.refs_0_, bf16[2048,256]{1,0:T(8,128)(2,1)S(1)} %collective-permute-done.4.refs_1_, ...), custom_call_target="tpu_custom_call" | custom-call | tf_op jit(solution)/shard_map/pallas_call | solution.py:192
  133.7 0.8 slice_bitcast_fusion
  134.5 1.5 collective-permute-start.18
  136.0 2.4 %collective-permute-start.19 = (s16[2,672,128]{2,1,0:T(8,128)(2,1)S(1)}, s16[2,672,128]{2,1,0:T(8,128)(2,1)S(1)}, u32[]{:S(2)}, u32[]{:S(2)}) collective-permute-start(s16[2,672,128]{2,1,0:T(8,128)(2,1)S(1)} %get-tuple-element.35), channel_id=1, source_target_pairs={{0,64},{1,65},{2,66},{3,67},{4,68},{5,69},{6,70},{7,71},{8,72},{9,... | collective-permute-start | bytes 1032200 | tf_op jit(solution)/shard_map/ppermute | solution.py:60
  138.4 1.2 collective-permute-start.20
  139.5 6.5 %collective-permute-done.18.refs_2_ = s16[2,672,128]{2,1,0:T(8,128)(2,1)S(1)} collective-permute-done((s16[2,672,128]{2,1,0:T(8,128)(2,1)}, s16[2,672,128]{2,1,0:T(8,128)(2,1)S(1)}, u32[]{:S(2)}, u32[]{:S(2)}) %collective-permute-start.18) | collective-permute-done | bytes 344096 | tf_op jit(solution)/shard_map/ppermute | solution.py:60
  146.1 7.4 %collective-permute-done.19.refs_3_ = s16[2,672,128]{2,1,0:T(8,128)(2,1)S(1)} collective-permute-done((s16[2,672,128]{2,1,0:T(8,128)(2,1)S(1)}, s16[2,672,128]{2,1,0:T(8,128)(2,1)S(1)}, u32[]{:S(2)}, u32[]{:S(2)}) %collective-permute-start.19) | collective-permute-done | bytes 344096 | tf_op jit(solution)/shard_map/ppermute | solution.py:60
  153.5 1.8 %shard_map.56 = (f32[512,640]{1,0:T(8,128)}, f32[16,128]{1,0:T(8,128)S(1)}) custom-call(s16[4,2,656,128]{3,2,1,0:T(8,128)(2,1)S(1)} %all-to-all-done.1.refs_0_, s16[2,672,128]{2,1,0:T(8,128)(2,1)S(1)} %get-tuple-element.37.refs_1_, s16[2,672,128]{2,1,0:T(8,128)(2,1)S(1)} %collective-permute-done.18.refs_2_, ...), custom_call_target="tpu_custom_call" | custom-call | tf_op jit(solution)/shard_map/pallas_call | solution.py:192
  155.3 0.6 slice_bitcast_fusion.4
  (27 shorter events, 0.1 us)
Async XLA Ops:
  0.6 13.8 %copy-start.15 = (s32[16]{0:T(128)S(1)}, s32[16]{0:T(128)}, u32[]{:S(2)}) copy-start(s32[16]{0:T(128)} %param.5) | copy-start | bytes 196
  0.7 1.6 %copy-start.1 = (bf16[1024,1024]{1,0:T(8,128)(2,1)S(1)}, bf16[1024,1024]{1,0:T(8,128)(2,1)}, u32[]{:S(2)}) copy-start(bf16[1024,1024]{1,0:T(8,128)(2,1)} %activations.1) | copy-start | bytes 6291460
  2.3 12.6 %copy-start.2 = (bf16[1024,640]{1,0:T(8,128)(2,1)S(1)}, bf16[1024,640]{1,0:T(8,128)(2,1)}, u32[]{:S(2)}) copy-start(bf16[1024,640]{1,0:T(8,128)(2,1)} %out_grad) | copy-start | bytes 3932164
  4.5 17.5 %collective-permute-start = (bf16[1024,256]{1,0:T(8,128)(2,1)}, bf16[1024,256]{1,0:T(8,128)(2,1)S(1)}, u32[]{:S(2)}, u32[]{:S(2)}) collective-permute-start(bf16[1024,256]{1,0:T(8,128)(2,1)} %get-tuple-element.17), channel_id=1, source_target_pairs={{0,0},{1,17},{2,2},{3,19},{4,4},{5,21},{6,6},{7,23},{8,8},{9,25},{... | collective-permute-start | bytes 1572872 | tf_op jit(solution)/shard_map/ppermute | solution.py:60
  10.0 14.9 %collective-permute-start.1 = (bf16[1024,256]{1,0:T(8,128)(2,1)}, bf16[1024,256]{1,0:T(8,128)(2,1)S(1)}, u32[]{:S(2)}, u32[]{:S(2)}) collective-permute-start(bf16[1024,256]{1,0:T(8,128)(2,1)} %get-tuple-element.18), channel_id=1, source_target_pairs={{0,8},{1,25},{2,10},{3,27},{4,12},{5,29},{6,14},{7,31},{8,1},{9,16... | collective-permute-start | bytes 1572872 | tf_op jit(solution)/shard_map/ppermute | solution.py:60
  10.5 22.4 %collective-permute-start.2 = (bf16[1024,256]{1,0:T(8,128)(2,1)}, bf16[1024,256]{1,0:T(8,128)(2,1)S(1)}, u32[]{:S(2)}, u32[]{:S(2)}) collective-permute-start(bf16[1024,256]{1,0:T(8,128)(2,1)} %get-tuple-element.19), channel_id=1, source_target_pairs={{0,0},{1,17},{2,2},{3,19},{4,4},{5,21},{6,6},{7,23},{8,8},{9,25},{... | collective-permute-start | bytes 1572872 | tf_op jit(solution)/shard_map/ppermute | solution.py:60
  14.3 20.0 %collective-permute-start.3 = (bf16[1024,256]{1,0:T(8,128)(2,1)}, bf16[1024,256]{1,0:T(8,128)(2,1)S(1)}, u32[]{:S(2)}, u32[]{:S(2)}) collective-permute-start(bf16[1024,256]{1,0:T(8,128)(2,1)} %get-tuple-element.20), channel_id=1, source_target_pairs={{0,8},{1,25},{2,10},{3,27},{4,12},{5,29},{6,14},{7,31},{8,1},{9,16... | collective-permute-start | bytes 1572872 | tf_op jit(solution)/shard_map/ppermute | solution.py:60
  16.2 2.4 %copy-start = (bf16[4,640,1024]{2,1,0:T(8,128)(2,1)}, bf16[4,640,1024]{2,1,0:T(8,128)(2,1)S(1)}, u32[]{:S(2)}) copy-start(bf16[4,640,1024]{2,1,0:T(8,128)(2,1)S(1)} %shard_map.51) | copy-start | bytes 15728644
  24.9 18.4 %collective-permute-start.7 = (bf16[2048,256]{1,0:T(8,128)(2,1)S(1)}, bf16[2048,256]{1,0:T(8,128)(2,1)}, u32[]{:S(2)}, u32[]{:S(2)}) collective-permute-start(bf16[2048,256]{1,0:T(8,128)(2,1)S(1)} %shard_map.52.refs_0_), channel_id=1, source_target_pairs={{0,2},{1,7},{2,4},{3,1},{4,6},{5,3},{6,0},{7,5},{8,10},{9,15},{10,... | collective-permute-start | bytes 3145736 | tf_op jit(solution)/shard_map/ppermute | solution.py:60
  34.4 65.1 %all-to-all-start = ((bf16[4,640,1024]{2,1,0:T(8,128)(2,1)}), bf16[4,640,1024]{2,1,0:T(8,128)(2,1)}, u32[]{:S(2)}, u32[]{:S(2)}) async-start(bf16[4,640,1024]{2,1,0:T(8,128)(2,1)} %copy-done), calls=%async_computation | async-start | bytes 10485760 | tf_op jit(solution)/shard_map/all_to_all | solution.py:64
  39.5 15.6 %collective-permute-start.4 = (bf16[2048,256]{1,0:T(8,128)(2,1)S(1)}, bf16[2048,256]{1,0:T(8,128)(2,1)S(1)}, u32[]{:S(2)}, u32[]{:S(2)}) collective-permute-start(bf16[2048,256]{1,0:T(8,128)(2,1)S(1)} %shard_map.53.refs_0_), channel_id=1, source_target_pairs={{0,2},{1,7},{2,4},{3,1},{4,6},{5,3},{6,0},{7,5},{8,10},{9,15},{10,... | collective-permute-start | bytes 3145736 | tf_op jit(solution)/shard_map/ppermute | solution.py:60
  43.3 11.7 %collective-permute-start.5 = (bf16[2048,256]{1,0:T(8,128)(2,1)S(1)}, bf16[2048,256]{1,0:T(8,128)(2,1)S(1)}, u32[]{:S(2)}, u32[]{:S(2)}) collective-permute-start(bf16[2048,256]{1,0:T(8,128)(2,1)S(1)} %shard_map.52.refs_0_), channel_id=1, source_target_pairs={{0,1},{1,0},{2,3},{3,2},{4,5},{5,4},{6,7},{7,6},{8,9},{9,8},{10,11... | collective-permute-start | bytes 3145736 | tf_op jit(solution)/shard_map/ppermute | solution.py:60
  43.3 23.1 %collective-permute-start.8 = (bf16[2048,256]{1,0:T(8,128)(2,1)}, bf16[2048,256]{1,0:T(8,128)(2,1)S(1)}, u32[]{:S(2)}, u32[]{:S(2)}) collective-permute-start(bf16[2048,256]{1,0:T(8,128)(2,1)} %collective-permute-done.7.refs_1_), channel_id=1, source_target_pairs={{0,2},{1,7},{2,4},{3,1},{4,6},{5,3},{6,0},{7,5},{8,10},{9,15},{10,... | collective-permute-start | bytes 3145736 | tf_op jit(solution)/shard_map/ppermute | solution.py:60
  44.3 22.1 %collective-permute-start.9 = (bf16[2048,256]{1,0:T(8,128)(2,1)}, bf16[2048,256]{1,0:T(8,128)(2,1)S(1)}, u32[]{:S(2)}, u32[]{:S(2)}) collective-permute-start(bf16[2048,256]{1,0:T(8,128)(2,1)} %collective-permute-done.7.refs_1_), channel_id=1, source_target_pairs={{0,1},{1,0},{2,3},{3,2},{4,5},{5,4},{6,7},{7,6},{8,9},{9,8},{10,11... | collective-permute-start | bytes 3145736 | tf_op jit(solution)/shard_map/ppermute | solution.py:60
  44.3 41.3 %collective-permute-start.13 = (bf16[2048,256]{1,0:T(8,128)(2,1)S(1)}, bf16[2048,256]{1,0:T(8,128)(2,1)S(1)}, u32[]{:S(2)}, u32[]{:S(2)}) collective-permute-start(bf16[2048,256]{1,0:T(8,128)(2,1)S(1)} %shard_map.53.refs_0_), channel_id=1, source_target_pairs={{0,1},{1,0},{2,3},{3,2},{4,5},{5,4},{6,7},{7,6},{8,9},{9,8},{10,11... | collective-permute-start | bytes 3145736 | tf_op jit(solution)/shard_map/ppermute | solution.py:60
  55.1 1.0 copy-start.5
  66.4 1.0 copy-start.11
  67.4 15.2 %collective-permute-start.10 = (bf16[2048,256]{1,0:T(8,128)(2,1)S(1)}, bf16[2048,256]{1,0:T(8,128)(2,1)}, u32[]{:S(2)}, u32[]{:S(2)}) collective-permute-start(bf16[2048,256]{1,0:T(8,128)(2,1)S(1)} %collective-permute-done.8.refs_2_), channel_id=1, source_target_pairs={{0,2},{1,7},{2,4},{3,1},{4,6},{5,3},{6,0},{7,5},{8,10},{9,15},{10,... | collective-permute-start | bytes 3145736 | tf_op jit(solution)/shard_map/ppermute | solution.py:60
  70.8 23.0 %collective-permute-start.6 = (bf16[2048,256]{1,0:T(8,128)(2,1)S(1)}, bf16[2048,256]{1,0:T(8,128)(2,1)}, u32[]{:S(2)}, u32[]{:S(2)}) collective-permute-start(bf16[2048,256]{1,0:T(8,128)(2,1)S(1)} %collective-permute-done.4.refs_1_), channel_id=1, source_target_pairs={{0,2},{1,7},{2,4},{3,1},{4,6},{5,3},{6,0},{7,5},{8,10},{9,15},{10,... | collective-permute-start | bytes 3145736 | tf_op jit(solution)/shard_map/ppermute | solution.py:60
  70.8 22.9 %collective-permute-start.14 = (bf16[2048,256]{1,0:T(8,128)(2,1)S(1)}, bf16[2048,256]{1,0:T(8,128)(2,1)S(1)}, u32[]{:S(2)}, u32[]{:S(2)}) collective-permute-start(bf16[2048,256]{1,0:T(8,128)(2,1)S(1)} %collective-permute-done.4.refs_1_), channel_id=1, source_target_pairs={{0,1},{1,0},{2,3},{3,2},{4,5},{5,4},{6,7},{7,6},{8,9},{9,8},{10,11... | collective-permute-start | bytes 3145736 | tf_op jit(solution)/shard_map/ppermute | solution.py:60
  71.3 23.5 %collective-permute-start.11 = (bf16[2048,256]{1,0:T(8,128)(2,1)S(1)}, bf16[2048,256]{1,0:T(8,128)(2,1)S(1)}, u32[]{:S(2)}, u32[]{:S(2)}) collective-permute-start(bf16[2048,256]{1,0:T(8,128)(2,1)S(1)} %collective-permute-done.8.refs_2_), channel_id=1, source_target_pairs={{0,1},{1,0},{2,3},{3,2},{4,5},{5,4},{6,7},{7,6},{8,9},{9,8},{10,11... | collective-permute-start | bytes 3145736 | tf_op jit(solution)/shard_map/ppermute | solution.py:60
  71.3 1.0 copy-start.7
  82.5 16.9 %collective-permute-start.12 = (bf16[2048,256]{1,0:T(8,128)(2,1)}, bf16[2048,256]{1,0:T(8,128)(2,1)}, u32[]{:S(2)}, u32[]{:S(2)}) collective-permute-start(bf16[2048,256]{1,0:T(8,128)(2,1)} %collective-permute-done.10.refs_3_), channel_id=1, source_target_pairs={{0,1},{1,0},{2,3},{3,2},{4,5},{5,4},{6,7},{7,6},{8,9},{9,8},{10,11... | collective-permute-start | bytes 3145736 | tf_op jit(solution)/shard_map/ppermute | solution.py:60
  85.6 1.0 copy-start.3
  93.8 1.0 copy-start.9
  94.8 1.0 copy-start.13
  95.8 19.2 %collective-permute-start.15 = (bf16[2048,256]{1,0:T(8,128)(2,1)}, bf16[2048,256]{1,0:T(8,128)(2,1)}, u32[]{:S(2)}, u32[]{:S(2)}) collective-permute-start(bf16[2048,256]{1,0:T(8,128)(2,1)} %collective-permute-done.6.refs_2_), channel_id=1, source_target_pairs={{0,2},{1,7},{2,4},{3,1},{4,6},{5,3},{6,0},{7,5},{8,10},{9,15},{10,... | collective-permute-start | bytes 3145736 | tf_op jit(solution)/shard_map/ppermute | solution.py:60
  99.4 20.8 %collective-permute-start.16 = (bf16[2048,256]{1,0:T(8,128)(2,1)}, bf16[2048,256]{1,0:T(8,128)(2,1)}, u32[]{:S(2)}, u32[]{:S(2)}) collective-permute-start(bf16[2048,256]{1,0:T(8,128)(2,1)} %collective-permute-done.6.refs_2_), channel_id=1, source_target_pairs={{0,1},{1,0},{2,3},{3,2},{4,5},{5,4},{6,7},{7,6},{8,9},{9,8},{10,11... | collective-permute-start | bytes 3145736 | tf_op jit(solution)/shard_map/ppermute | solution.py:60
  99.5 1.2 copy-start.6
  100.7 1.2 copy-start.8
  101.9 1.2 copy-start.12
  103.1 1.2 copy-start.14
  115.0 5.3 %collective-permute-start.17 = (bf16[2048,256]{1,0:T(8,128)(2,1)}, bf16[2048,256]{1,0:T(8,128)(2,1)}, u32[]{:S(2)}, u32[]{:S(2)}) collective-permute-start(bf16[2048,256]{1,0:T(8,128)(2,1)} %collective-permute-done.15.refs_3_), channel_id=1, source_target_pairs={{0,1},{1,0},{2,3},{3,2},{4,5},{5,4},{6,7},{7,6},{8,9},{9,8},{10,11... | collective-permute-start | bytes 3145736 | tf_op jit(solution)/shard_map/ppermute | solution.py:60
  116.0 23.5 %all-to-all-start.1 = ((s16[4,2,656,128]{3,2,1,0:T(8,128)(2,1)}), s16[4,2,656,128]{3,2,1,0:T(8,128)(2,1)S(1)}, u32[]{:S(2)}, u32[]{:S(2)}) async-start(s16[4,2,656,128]{3,2,1,0:T(8,128)(2,1)} %shard_map.54), calls=%async_computation.1 | async-start | bytes 2686976 | tf_op jit(solution)/shard_map/all_to_all | solution.py:64
  120.2 1.2 copy-start.4
  121.5 1.2 copy-start.10
  134.5 11.6 %collective-permute-start.18 = (s16[2,672,128]{2,1,0:T(8,128)(2,1)}, s16[2,672,128]{2,1,0:T(8,128)(2,1)S(1)}, u32[]{:S(2)}, u32[]{:S(2)}) collective-permute-start(s16[2,672,128]{2,1,0:T(8,128)(2,1)} %get-tuple-element.36), channel_id=1, source_target_pairs={{0,32},{1,33},{2,34},{3,35},{4,36},{5,37},{6,38},{7,39},{8,40},{9,... | collective-permute-start | bytes 1032200 | tf_op jit(solution)/shard_map/ppermute | solution.py:60
  136.0 17.5 %collective-permute-start.19 = (s16[2,672,128]{2,1,0:T(8,128)(2,1)S(1)}, s16[2,672,128]{2,1,0:T(8,128)(2,1)S(1)}, u32[]{:S(2)}, u32[]{:S(2)}) collective-permute-start(s16[2,672,128]{2,1,0:T(8,128)(2,1)S(1)} %get-tuple-element.35), channel_id=1, source_target_pairs={{0,64},{1,65},{2,66},{3,67},{4,68},{5,69},{6,70},{7,71},{8,72},{9,... | collective-permute-start | bytes 1032200 | tf_op jit(solution)/shard_map/ppermute | solution.py:60
  138.4 15.2 %collective-permute-start.20 = (s16[2,672,128]{2,1,0:T(8,128)(2,1)S(1)}, s16[2,672,128]{2,1,0:T(8,128)(2,1)S(1)}, u32[]{:S(2)}, u32[]{:S(2)}) collective-permute-start(s16[2,672,128]{2,1,0:T(8,128)(2,1)S(1)} %get-tuple-element.34), channel_id=1, source_target_pairs={{0,96},{1,97},{2,98},{3,99},{4,100},{5,101},{6,102},{7,103},{8,104... | collective-permute-start | bytes 1032200 | tf_op jit(solution)/shard_map/ppermute | solution.py:60

commit v5 on v4

--- a/solution.py
+++ b/solution.py
@@ -249,7 +249,7 @@
     ring[1].append(send(after(ring[1][2], *other[1], other[0][2]), RING_Z))
     other[1].append(send(ring[1][2], SWAP))
     other[0].append(send(ring[0][3], SWAP))
-    early = sums(tables[0], grads, [after(ring[0][0], ring[1][2]), *ring[0][1:]], other[0], False)
+    early = sums(tables[0], grads, ring[0], other[0], False)
     other[1].append(send(after(ring[1][3], early), SWAP))
     late = sums(tables[1], grads, ring[1], other[1], True)
     messages = [

time: 157 us -> 157 us (level)
  no operation moved by 1% of the time
where the time goes in v5:
time: 157 us; the launch traced here: 156 us
  waiting for transfers between devices  65.5 us (42%)
  starting transfers between devices  43.5 us (28%)
  Pallas kernels  26.8 us (17%)
  local copies, waits for them, and re-layouts  19.2 us (12%)
    ppermute x21, waiting for transfers between devices, send(): return lax.ppermute(value, AXES, perm)  65.5 us
    ppermute x21, starting transfers between devices, send(): return lax.ppermute(value, AXES, perm)  34.3 us
    pallas_call x7, Pallas kernels, kernel(): pl.pallas_call(body, out_shape=out_shape, in_specs=[scalars()] * (scalar...  26.8 us
    unnamed x32, local copies, waits for them, and re-layouts  17.2 us
    all_to_all x2, starting transfers between devices, swap_all(): lax.all_to_all(value, AXES, 0, 0, axis_index_groups=groups, tiled=True)  9.27 us
  transfers between devices with their start and end apart: 23, of which 10 were waited for; matrix products, arithmetic and copies ran while one was open for 1% of the time, Pallas kernels for 15%

profile of v5, /device:TPU:1, one launch (start us, length us, event | category | flops | bytes accessed | tf_op | source)
XLA Modules:
  0.0 156.1 jit_solution(12146963591031800675)
XLA Ops:
  0.7 0.1 pad_add_fusion.1.halves
  0.7 1.6 %copy-done.1 = bf16[1024,1024]{1,0:T(8,128)(2,1)S(1)} copy-done((bf16[1024,1024]{1,0:T(8,128)(2,1)S(1)}, bf16[1024,1024]{1,0:T(8,128)(2,1)}, u32[]{:S(2)}) %copy-start.1) | copy-done | bytes 2097176
  2.3 2.2 %shard_map.50 = (bf16[1024,256]{1,0:T(8,128)(2,1)}, bf16[1024,256]{1,0:T(8,128)(2,1)}, bf16[1024,256]{1,0:T(8,128)(2,1)}, bf16[1024,256]{1,0:T(8,128)(2,1)}) custom-call(s32[2]{0:T(128)S(1)} %pad_add_fusion.1.halves, bf16[1024,1024]{1,0:T(8,128)(2,1)S(1)} %copy-done.1), custom_call_target="tpu_custom_call" | custom-call | tf_op jit(solution)/shard_map/pallas_call | solution.py:192
  4.5 5.5 %collective-permute-start = (bf16[1024,256]{1,0:T(8,128)(2,1)}, bf16[1024,256]{1,0:T(8,128)(2,1)S(1)}, u32[]{:S(2)}, u32[]{:S(2)}) collective-permute-start(bf16[1024,256]{1,0:T(8,128)(2,1)} %get-tuple-element.16), channel_id=1, source_target_pairs={{0,0},{1,17},{2,2},{3,19},{4,4},{5,21},{6,6},{7,23},{8,8},{9,25},{... | collective-permute-start | bytes 1572872 | tf_op jit(solution)/shard_map/ppermute | solution.py:60
  10.0 0.5 collective-permute-start.1
  10.5 3.8 %collective-permute-start.2 = (bf16[1024,256]{1,0:T(8,128)(2,1)}, bf16[1024,256]{1,0:T(8,128)(2,1)S(1)}, u32[]{:S(2)}, u32[]{:S(2)}) collective-permute-start(bf16[1024,256]{1,0:T(8,128)(2,1)} %get-tuple-element.18), channel_id=1, source_target_pairs={{0,0},{1,17},{2,2},{3,19},{4,4},{5,21},{6,6},{7,23},{8,8},{9,25},{... | collective-permute-start | bytes 1572872 | tf_op jit(solution)/shard_map/ppermute | solution.py:60
  14.3 0.1 collective-permute-start.3
  14.4 0.6 dynamic_slice.3.count
  15.0 1.2 shard_map.51
  16.2 2.4 %copy-done = bf16[4,640,1024]{2,1,0:T(8,128)(2,1)} copy-done((bf16[4,640,1024]{2,1,0:T(8,128)(2,1)}, bf16[4,640,1024]{2,1,0:T(8,128)(2,1)S(1)}, u32[]{:S(2)}) %copy-start) | copy-done | bytes 5242904
  18.6 3.4 %collective-permute-done.near = bf16[1024,256]{1,0:T(8,128)(2,1)S(1)} collective-permute-done((bf16[1024,256]{1,0:T(8,128)(2,1)}, bf16[1024,256]{1,0:T(8,128)(2,1)S(1)}, u32[]{:S(2)}, u32[]{:S(2)}) %collective-permute-start) | collective-permute-done | bytes 524320 | tf_op jit(solution)/shard_map/ppermute | solution.py:60
  22.0 2.9 %collective-permute-done.1.far = bf16[1024,256]{1,0:T(8,128)(2,1)S(1)} collective-permute-done((bf16[1024,256]{1,0:T(8,128)(2,1)}, bf16[1024,256]{1,0:T(8,128)(2,1)S(1)}, u32[]{:S(2)}, u32[]{:S(2)}) %collective-permute-start.1) | collective-permute-done | bytes 524320 | tf_op jit(solution)/shard_map/ppermute | solution.py:60
  24.9 0.1 shard_map.52.refs_0_
  24.9 3.8 %collective-permute-start.4 = (bf16[2048,256]{1,0:T(8,128)(2,1)S(1)}, bf16[2048,256]{1,0:T(8,128)(2,1)}, u32[]{:S(2)}, u32[]{:S(2)}) collective-permute-start(bf16[2048,256]{1,0:T(8,128)(2,1)S(1)} %shard_map.52.refs_0_), channel_id=1, source_target_pairs={{0,2},{1,7},{2,4},{3,1},{4,6},{5,3},{6,0},{7,5},{8,10},{9,15},{10,... | collective-permute-start | bytes 3145736 | tf_op jit(solution)/shard_map/ppermute | solution.py:60
  28.8 4.1 %collective-permute-done.2.near = bf16[1024,256]{1,0:T(8,128)(2,1)S(1)} collective-permute-done((bf16[1024,256]{1,0:T(8,128)(2,1)}, bf16[1024,256]{1,0:T(8,128)(2,1)S(1)}, u32[]{:S(2)}, u32[]{:S(2)}) %collective-permute-start.2) | collective-permute-done | bytes 524320 | tf_op jit(solution)/shard_map/ppermute | solution.py:60
  32.8 1.5 collective-permute-done.3.far
  34.3 0.1 shard_map.53.refs_0_
  34.4 5.1 %all-to-all-start = ((bf16[4,640,1024]{2,1,0:T(8,128)(2,1)}), bf16[4,640,1024]{2,1,0:T(8,128)(2,1)}, u32[]{:S(2)}, u32[]{:S(2)}) async-start(bf16[4,640,1024]{2,1,0:T(8,128)(2,1)} %copy-done), calls=%async_computation | async-start | bytes 10485760 | tf_op jit(solution)/shard_map/all_to_all | solution.py:64
  39.5 0.9 collective-permute-start.8
  40.4 3.8 %collective-permute-start.11 = (bf16[2048,256]{1,0:T(8,128)(2,1)S(1)}, bf16[2048,256]{1,0:T(8,128)(2,1)S(1)}, u32[]{:S(2)}, u32[]{:S(2)}) collective-permute-start(bf16[2048,256]{1,0:T(8,128)(2,1)S(1)} %shard_map.53.refs_0_), channel_id=1, source_target_pairs={{0,2},{1,7},{2,4},{3,1},{4,6},{5,3},{6,0},{7,5},{8,10},{9,15},{10,... | collective-permute-start | bytes 3145736 | tf_op jit(solution)/shard_map/ppermute | solution.py:60
  44.2 0.0 collective-permute-done.4.refs_1_
  44.2 0.1 collective-permute-start.5
  44.3 0.0 collective-permute-start.6
  44.3 0.5 collective-permute-start.13
  44.8 1.0 copy-done.5
  45.8 10.1 %collective-permute-done.11.refs_1_ = bf16[2048,256]{1,0:T(8,128)(2,1)S(1)} collective-permute-done((bf16[2048,256]{1,0:T(8,128)(2,1)S(1)}, bf16[2048,256]{1,0:T(8,128)(2,1)S(1)}, u32[]{:S(2)}, u32[]{:S(2)}) %collective-permute-start.11) | collective-permute-done | bytes 1048608 | tf_op jit(solution)/shard_map/ppermute | solution.py:60
  55.9 11.3 %collective-permute-done.5.refs_2_ = bf16[2048,256]{1,0:T(8,128)(2,1)S(1)} collective-permute-done((bf16[2048,256]{1,0:T(8,128)(2,1)}, bf16[2048,256]{1,0:T(8,128)(2,1)S(1)}, u32[]{:S(2)}, u32[]{:S(2)}) %collective-permute-start.5) | collective-permute-done | bytes 1048608 | tf_op jit(solution)/shard_map/ppermute | solution.py:60
  67.3 1.0 copy-done.11
  68.2 3.4 %collective-permute-start.7 = (bf16[2048,256]{1,0:T(8,128)(2,1)S(1)}, bf16[2048,256]{1,0:T(8,128)(2,1)}, u32[]{:S(2)}, u32[]{:S(2)}) collective-permute-start(bf16[2048,256]{1,0:T(8,128)(2,1)S(1)} %collective-permute-done.5.refs_2_), channel_id=1, source_target_pairs={{0,2},{1,7},{2,4},{3,1},{4,6},{5,3},{6,0},{7,5},{8,10},{9,15},{10,... | collective-permute-start | bytes 3145736 | tf_op jit(solution)/shard_map/ppermute | solution.py:60
  71.7 0.0 collective-permute-start.12
  71.7 0.5 collective-permute-start.9
  72.2 1.0 copy-done.7
  73.2 10.2 %collective-permute-done.7.refs_3_ = bf16[2048,256]{1,0:T(8,128)(2,1)} collective-permute-done((bf16[2048,256]{1,0:T(8,128)(2,1)S(1)}, bf16[2048,256]{1,0:T(8,128)(2,1)}, u32[]{:S(2)}, u32[]{:S(2)}) %collective-permute-start.7) | collective-permute-done | bytes 1048608 | tf_op jit(solution)/shard_map/ppermute | solution.py:60
  83.4 2.3 %collective-permute-start.10 = (bf16[2048,256]{1,0:T(8,128)(2,1)}, bf16[2048,256]{1,0:T(8,128)(2,1)}, u32[]{:S(2)}, u32[]{:S(2)}) collective-permute-start(bf16[2048,256]{1,0:T(8,128)(2,1)} %collective-permute-done.7.refs_3_), channel_id=1, source_target_pairs={{0,1},{1,0},{2,3},{3,2},{4,5},{5,4},{6,7},{7,6},{8,9},{9,8},{10,11... | collective-permute-start | bytes 3145736 | tf_op jit(solution)/shard_map/ppermute | solution.py:60
  85.6 0.0 collective-permute-done.13.refs_4_
  85.7 1.0 copy-done.3
  86.6 8.0 %collective-permute-done.12.refs_2_ = bf16[2048,256]{1,0:T(8,128)(2,1)} collective-permute-done((bf16[2048,256]{1,0:T(8,128)(2,1)S(1)}, bf16[2048,256]{1,0:T(8,128)(2,1)}, u32[]{:S(2)}, u32[]{:S(2)}) %collective-permute-start.12) | collective-permute-done | bytes 1048608 | tf_op jit(solution)/shard_map/ppermute | solution.py:60
  94.6 0.0 collective-permute-done.14.refs_5_
  94.6 1.0 copy-done.9
  95.6 0.0 collective-permute-done.9.refs_6_
  95.6 1.0 copy-done.13
  96.6 3.5 %collective-permute-start.15 = (bf16[2048,256]{1,0:T(8,128)(2,1)}, bf16[2048,256]{1,0:T(8,128)(2,1)}, u32[]{:S(2)}, u32[]{:S(2)}) collective-permute-start(bf16[2048,256]{1,0:T(8,128)(2,1)} %collective-permute-done.12.refs_2_), channel_id=1, source_target_pairs={{0,2},{1,7},{2,4},{3,1},{4,6},{5,3},{6,0},{7,5},{8,10},{9,15},{10,... | collective-permute-start | bytes 3145736 | tf_op jit(solution)/shard_map/ppermute | solution.py:60
  100.2 0.1 pad_add_fusion.2
  100.3 0.0 collective-permute-start.16
  100.3 0.0 all-to-all-done.grads
  100.3 0.0 collective-permute-done.10.refs_7_
  100.3 1.2 copy-done.6
  101.5 1.2 copy-done.8
  102.8 1.2 copy-done.12
  104.0 1.2 copy-done.14
  105.2 10.6 %shard_map.54 = s16[4,2,656,128]{3,2,1,0:T(8,128)(2,1)} custom-call(s32[8]{0:T(128)S(1)} %get-tuple-element.37.table, bf16[4,640,1024]{2,1,0:T(8,128)(2,1)} %all-to-all-done.grads, bf16[2048,256]{1,0:T(8,128)(2,1)S(1)} %shard_map.52.refs_0_, bf16[2048,256]{1,0:T(8,128)(2,1)} %collective-permute-done.4.refs_1_, bf16[2048,256]{1,0:T(8,128)(2,1)S(1)} %copy-done.8, ...), custom_call_target="tpu_custom_call" | custom-call | tf_op jit(solution)/shard_map/pallas_call | solution.py:192
  115.8 0.5 collective-permute-start.17
  116.3 4.2 %all-to-all-start.1 = ((s16[4,2,656,128]{3,2,1,0:T(8,128)(2,1)}), s16[4,2,656,128]{3,2,1,0:T(8,128)(2,1)S(1)}, u32[]{:S(2)}, u32[]{:S(2)}) async-start(s16[4,2,656,128]{3,2,1,0:T(8,128)(2,1)} %shard_map.54), calls=%async_computation.1 | async-start | bytes 2686976 | tf_op jit(solution)/shard_map/all_to_all | solution.py:64
  120.5 1.2 copy-done.4
  121.7 1.2 copy-done.10
  122.9 11.0 %shard_map.55 = s16[4,2,672,128]{3,2,1,0:T(8,128)(2,1)S(1)} custom-call(s32[8]{0:T(128)S(1)} %get-tuple-element.36.table, bf16[4,640,1024]{2,1,0:T(8,128)(2,1)} %all-to-all-done.grads, bf16[2048,256]{1,0:T(8,128)(2,1)S(1)} %shard_map.53.refs_0_, bf16[2048,256]{1,0:T(8,128)(2,1)S(1)} %collective-permute-done.11.refs_1_, ...), custom_call_target="tpu_custom_call" | custom-call | tf_op jit(solution)/shard_map/pallas_call | solution.py:192
  133.9 0.8 slice_bitcast_fusion
  134.7 1.5 collective-permute-start.18
  136.2 2.4 %collective-permute-start.19 = (s16[2,672,128]{2,1,0:T(8,128)(2,1)S(1)}, s16[2,672,128]{2,1,0:T(8,128)(2,1)S(1)}, u32[]{:S(2)}, u32[]{:S(2)}) collective-permute-start(s16[2,672,128]{2,1,0:T(8,128)(2,1)S(1)} %get-tuple-element.33), channel_id=1, source_target_pairs={{0,64},{1,65},{2,66},{3,67},{4,68},{5,69},{6,70},{7,71},{8,72},{9,... | collective-permute-start | bytes 1032200 | tf_op jit(solution)/shard_map/ppermute | solution.py:60
  138.6 1.2 collective-permute-start.20
  139.8 6.5 %collective-permute-done.18.refs_2_ = s16[2,672,128]{2,1,0:T(8,128)(2,1)S(1)} collective-permute-done((s16[2,672,128]{2,1,0:T(8,128)(2,1)}, s16[2,672,128]{2,1,0:T(8,128)(2,1)S(1)}, u32[]{:S(2)}, u32[]{:S(2)}) %collective-permute-start.18) | collective-permute-done | bytes 344096 | tf_op jit(solution)/shard_map/ppermute | solution.py:60
  146.3 7.4 %collective-permute-done.19.refs_3_ = s16[2,672,128]{2,1,0:T(8,128)(2,1)S(1)} collective-permute-done((s16[2,672,128]{2,1,0:T(8,128)(2,1)S(1)}, s16[2,672,128]{2,1,0:T(8,128)(2,1)S(1)}, u32[]{:S(2)}, u32[]{:S(2)}) %collective-permute-start.19) | collective-permute-done | bytes 344096 | tf_op jit(solution)/shard_map/ppermute | solution.py:60
  153.8 1.8 %shard_map.56 = (f32[512,640]{1,0:T(8,128)}, f32[16,128]{1,0:T(8,128)S(1)}) custom-call(s16[4,2,656,128]{3,2,1,0:T(8,128)(2,1)S(1)} %all-to-all-done.1.refs_0_, s16[2,672,128]{2,1,0:T(8,128)(2,1)S(1)} %get-tuple-element.35.refs_1_, s16[2,672,128]{2,1,0:T(8,128)(2,1)S(1)} %collective-permute-done.18.refs_2_, ...), custom_call_target="tpu_custom_call" | custom-call | tf_op jit(solution)/shard_map/pallas_call | solution.py:192
  155.5 0.6 slice_bitcast_fusion.4
  (27 shorter events, 0.1 us)
Async XLA Ops:
  0.6 13.8 %copy-start.15 = (s32[16]{0:T(128)S(1)}, s32[16]{0:T(128)}, u32[]{:S(2)}) copy-start(s32[16]{0:T(128)} %param.5) | copy-start | bytes 196
  0.7 1.6 %copy-start.1 = (bf16[1024,1024]{1,0:T(8,128)(2,1)S(1)}, bf16[1024,1024]{1,0:T(8,128)(2,1)}, u32[]{:S(2)}) copy-start(bf16[1024,1024]{1,0:T(8,128)(2,1)} %activations.1) | copy-start | bytes 6291460
  2.3 12.6 %copy-start.2 = (bf16[1024,640]{1,0:T(8,128)(2,1)S(1)}, bf16[1024,640]{1,0:T(8,128)(2,1)}, u32[]{:S(2)}) copy-start(bf16[1024,640]{1,0:T(8,128)(2,1)} %out_grad) | copy-start | bytes 3932164
  4.5 17.5 %collective-permute-start = (bf16[1024,256]{1,0:T(8,128)(2,1)}, bf16[1024,256]{1,0:T(8,128)(2,1)S(1)}, u32[]{:S(2)}, u32[]{:S(2)}) collective-permute-start(bf16[1024,256]{1,0:T(8,128)(2,1)} %get-tuple-element.16), channel_id=1, source_target_pairs={{0,0},{1,17},{2,2},{3,19},{4,4},{5,21},{6,6},{7,23},{8,8},{9,25},{... | collective-permute-start | bytes 1572872 | tf_op jit(solution)/shard_map/ppermute | solution.py:60
  10.0 14.9 %collective-permute-start.1 = (bf16[1024,256]{1,0:T(8,128)(2,1)}, bf16[1024,256]{1,0:T(8,128)(2,1)S(1)}, u32[]{:S(2)}, u32[]{:S(2)}) collective-permute-start(bf16[1024,256]{1,0:T(8,128)(2,1)} %get-tuple-element.17), channel_id=1, source_target_pairs={{0,8},{1,25},{2,10},{3,27},{4,12},{5,29},{6,14},{7,31},{8,1},{9,16... | collective-permute-start | bytes 1572872 | tf_op jit(solution)/shard_map/ppermute | solution.py:60
  10.5 22.4 %collective-permute-start.2 = (bf16[1024,256]{1,0:T(8,128)(2,1)}, bf16[1024,256]{1,0:T(8,128)(2,1)S(1)}, u32[]{:S(2)}, u32[]{:S(2)}) collective-permute-start(bf16[1024,256]{1,0:T(8,128)(2,1)} %get-tuple-element.18), channel_id=1, source_target_pairs={{0,0},{1,17},{2,2},{3,19},{4,4},{5,21},{6,6},{7,23},{8,8},{9,25},{... | collective-permute-start | bytes 1572872 | tf_op jit(solution)/shard_map/ppermute | solution.py:60
  14.3 20.0 %collective-permute-start.3 = (bf16[1024,256]{1,0:T(8,128)(2,1)}, bf16[1024,256]{1,0:T(8,128)(2,1)S(1)}, u32[]{:S(2)}, u32[]{:S(2)}) collective-permute-start(bf16[1024,256]{1,0:T(8,128)(2,1)} %get-tuple-element.19), channel_id=1, source_target_pairs={{0,8},{1,25},{2,10},{3,27},{4,12},{5,29},{6,14},{7,31},{8,1},{9,16... | collective-permute-start | bytes 1572872 | tf_op jit(solution)/shard_map/ppermute | solution.py:60
  16.2 2.4 %copy-start = (bf16[4,640,1024]{2,1,0:T(8,128)(2,1)}, bf16[4,640,1024]{2,1,0:T(8,128)(2,1)S(1)}, u32[]{:S(2)}) copy-start(bf16[4,640,1024]{2,1,0:T(8,128)(2,1)S(1)} %shard_map.51) | copy-start | bytes 15728644
  24.9 19.2 %collective-permute-start.4 = (bf16[2048,256]{1,0:T(8,128)(2,1)S(1)}, bf16[2048,256]{1,0:T(8,128)(2,1)}, u32[]{:S(2)}, u32[]{:S(2)}) collective-permute-start(bf16[2048,256]{1,0:T(8,128)(2,1)S(1)} %shard_map.52.refs_0_), channel_id=1, source_target_pairs={{0,2},{1,7},{2,4},{3,1},{4,6},{5,3},{6,0},{7,5},{8,10},{9,15},{10,... | collective-permute-start | bytes 3145736 | tf_op jit(solution)/shard_map/ppermute | solution.py:60
  34.4 65.9 %all-to-all-start = ((bf16[4,640,1024]{2,1,0:T(8,128)(2,1)}), bf16[4,640,1024]{2,1,0:T(8,128)(2,1)}, u32[]{:S(2)}, u32[]{:S(2)}) async-start(bf16[4,640,1024]{2,1,0:T(8,128)(2,1)} %copy-done), calls=%async_computation | async-start | bytes 10485760 | tf_op jit(solution)/shard_map/all_to_all | solution.py:64
  39.5 5.3 %collective-permute-start.8 = (bf16[2048,256]{1,0:T(8,128)(2,1)S(1)}, bf16[2048,256]{1,0:T(8,128)(2,1)S(1)}, u32[]{:S(2)}, u32[]{:S(2)}) collective-permute-start(bf16[2048,256]{1,0:T(8,128)(2,1)S(1)} %shard_map.52.refs_0_), channel_id=1, source_target_pairs={{0,1},{1,0},{2,3},{3,2},{4,5},{5,4},{6,7},{7,6},{8,9},{9,8},{10,11... | collective-permute-start | bytes 3145736 | tf_op jit(solution)/shard_map/ppermute | solution.py:60
  40.4 15.5 %collective-permute-start.11 = (bf16[2048,256]{1,0:T(8,128)(2,1)S(1)}, bf16[2048,256]{1,0:T(8,128)(2,1)S(1)}, u32[]{:S(2)}, u32[]{:S(2)}) collective-permute-start(bf16[2048,256]{1,0:T(8,128)(2,1)S(1)} %shard_map.53.refs_0_), channel_id=1, source_target_pairs={{0,2},{1,7},{2,4},{3,1},{4,6},{5,3},{6,0},{7,5},{8,10},{9,15},{10,... | collective-permute-start | bytes 3145736 | tf_op jit(solution)/shard_map/ppermute | solution.py:60
  44.2 23.1 %collective-permute-start.5 = (bf16[2048,256]{1,0:T(8,128)(2,1)}, bf16[2048,256]{1,0:T(8,128)(2,1)S(1)}, u32[]{:S(2)}, u32[]{:S(2)}) collective-permute-start(bf16[2048,256]{1,0:T(8,128)(2,1)} %collective-permute-done.4.refs_1_), channel_id=1, source_target_pairs={{0,2},{1,7},{2,4},{3,1},{4,6},{5,3},{6,0},{7,5},{8,10},{9,15},{10,... | collective-permute-start | bytes 3145736 | tf_op jit(solution)/shard_map/ppermute | solution.py:60
  44.3 23.0 %collective-permute-start.6 = (bf16[2048,256]{1,0:T(8,128)(2,1)}, bf16[2048,256]{1,0:T(8,128)(2,1)S(1)}, u32[]{:S(2)}, u32[]{:S(2)}) collective-permute-start(bf16[2048,256]{1,0:T(8,128)(2,1)} %collective-permute-done.4.refs_1_), channel_id=1, source_target_pairs={{0,1},{1,0},{2,3},{3,2},{4,5},{5,4},{6,7},{7,6},{8,9},{9,8},{10,11... | collective-permute-start | bytes 3145736 | tf_op jit(solution)/shard_map/ppermute | solution.py:60
  44.3 41.3 %collective-permute-start.13 = (bf16[2048,256]{1,0:T(8,128)(2,1)S(1)}, bf16[2048,256]{1,0:T(8,128)(2,1)S(1)}, u32[]{:S(2)}, u32[]{:S(2)}) collective-permute-start(bf16[2048,256]{1,0:T(8,128)(2,1)S(1)} %shard_map.53.refs_0_), channel_id=1, source_target_pairs={{0,1},{1,0},{2,3},{3,2},{4,5},{5,4},{6,7},{7,6},{8,9},{9,8},{10,11... | collective-permute-start | bytes 3145736 | tf_op jit(solution)/shard_map/ppermute | solution.py:60
  44.8 1.0 copy-start.5
  67.3 1.0 copy-start.11
  68.2 15.2 %collective-permute-start.7 = (bf16[2048,256]{1,0:T(8,128)(2,1)S(1)}, bf16[2048,256]{1,0:T(8,128)(2,1)}, u32[]{:S(2)}, u32[]{:S(2)}) collective-permute-start(bf16[2048,256]{1,0:T(8,128)(2,1)S(1)} %collective-permute-done.5.refs_2_), channel_id=1, source_target_pairs={{0,2},{1,7},{2,4},{3,1},{4,6},{5,3},{6,0},{7,5},{8,10},{9,15},{10,... | collective-permute-start | bytes 3145736 | tf_op jit(solution)/shard_map/ppermute | solution.py:60
  71.7 23.0 %collective-permute-start.12 = (bf16[2048,256]{1,0:T(8,128)(2,1)S(1)}, bf16[2048,256]{1,0:T(8,128)(2,1)}, u32[]{:S(2)}, u32[]{:S(2)}) collective-permute-start(bf16[2048,256]{1,0:T(8,128)(2,1)S(1)} %collective-permute-done.11.refs_1_), channel_id=1, source_target_pairs={{0,2},{1,7},{2,4},{3,1},{4,6},{5,3},{6,0},{7,5},{8,10},{9,15},{10,... | collective-permute-start | bytes 3145736 | tf_op jit(solution)/shard_map/ppermute | solution.py:60
  71.7 22.9 %collective-permute-start.14 = (bf16[2048,256]{1,0:T(8,128)(2,1)S(1)}, bf16[2048,256]{1,0:T(8,128)(2,1)S(1)}, u32[]{:S(2)}, u32[]{:S(2)}) collective-permute-start(bf16[2048,256]{1,0:T(8,128)(2,1)S(1)} %collective-permute-done.11.refs_1_), channel_id=1, source_target_pairs={{0,1},{1,0},{2,3},{3,2},{4,5},{5,4},{6,7},{7,6},{8,9},{9,8},{10,11... | collective-permute-start | bytes 3145736 | tf_op jit(solution)/shard_map/ppermute | solution.py:60
  71.7 23.9 %collective-permute-start.9 = (bf16[2048,256]{1,0:T(8,128)(2,1)S(1)}, bf16[2048,256]{1,0:T(8,128)(2,1)S(1)}, u32[]{:S(2)}, u32[]{:S(2)}) collective-permute-start(bf16[2048,256]{1,0:T(8,128)(2,1)S(1)} %collective-permute-done.5.refs_2_), channel_id=1, source_target_pairs={{0,1},{1,0},{2,3},{3,2},{4,5},{5,4},{6,7},{7,6},{8,9},{9,8},{10,11... | collective-permute-start | bytes 3145736 | tf_op jit(solution)/shard_map/ppermute | solution.py:60
  72.2 1.0 copy-start.7
  83.4 16.9 %collective-permute-start.10 = (bf16[2048,256]{1,0:T(8,128)(2,1)}, bf16[2048,256]{1,0:T(8,128)(2,1)}, u32[]{:S(2)}, u32[]{:S(2)}) collective-permute-start(bf16[2048,256]{1,0:T(8,128)(2,1)} %collective-permute-done.7.refs_3_), channel_id=1, source_target_pairs={{0,1},{1,0},{2,3},{3,2},{4,5},{5,4},{6,7},{7,6},{8,9},{9,8},{10,11... | collective-permute-start | bytes 3145736 | tf_op jit(solution)/shard_map/ppermute | solution.py:60
  85.7 1.0 copy-start.3
  94.6 1.0 copy-start.9
  95.6 1.0 copy-start.13
  96.6 19.2 %collective-permute-start.15 = (bf16[2048,256]{1,0:T(8,128)(2,1)}, bf16[2048,256]{1,0:T(8,128)(2,1)}, u32[]{:S(2)}, u32[]{:S(2)}) collective-permute-start(bf16[2048,256]{1,0:T(8,128)(2,1)} %collective-permute-done.12.refs_2_), channel_id=1, source_target_pairs={{0,2},{1,7},{2,4},{3,1},{4,6},{5,3},{6,0},{7,5},{8,10},{9,15},{10,... | collective-permute-start | bytes 3145736 | tf_op jit(solution)/shard_map/ppermute | solution.py:60
  100.3 20.2 %collective-permute-start.16 = (bf16[2048,256]{1,0:T(8,128)(2,1)}, bf16[2048,256]{1,0:T(8,128)(2,1)}, u32[]{:S(2)}, u32[]{:S(2)}) collective-permute-start(bf16[2048,256]{1,0:T(8,128)(2,1)} %collective-permute-done.12.refs_2_), channel_id=1, source_target_pairs={{0,1},{1,0},{2,3},{3,2},{4,5},{5,4},{6,7},{7,6},{8,9},{9,8},{10,11... | collective-permute-start | bytes 3145736 | tf_op jit(solution)/shard_map/ppermute | solution.py:60
  100.3 1.2 copy-start.6
  101.5 1.2 copy-start.8
  102.8 1.2 copy-start.12
  104.0 1.2 copy-start.14
  115.8 4.7 %collective-permute-start.17 = (bf16[2048,256]{1,0:T(8,128)(2,1)}, bf16[2048,256]{1,0:T(8,128)(2,1)}, u32[]{:S(2)}, u32[]{:S(2)}) collective-permute-start(bf16[2048,256]{1,0:T(8,128)(2,1)} %collective-permute-done.15.refs_3_), channel_id=1, source_target_pairs={{0,1},{1,0},{2,3},{3,2},{4,5},{5,4},{6,7},{7,6},{8,9},{9,8},{10,11... | collective-permute-start | bytes 3145736 | tf_op jit(solution)/shard_map/ppermute | solution.py:60
  116.3 23.5 %all-to-all-start.1 = ((s16[4,2,656,128]{3,2,1,0:T(8,128)(2,1)}), s16[4,2,656,128]{3,2,1,0:T(8,128)(2,1)S(1)}, u32[]{:S(2)}, u32[]{:S(2)}) async-start(s16[4,2,656,128]{3,2,1,0:T(8,128)(2,1)} %shard_map.54), calls=%async_computation.1 | async-start | bytes 2686976 | tf_op jit(solution)/shard_map/all_to_all | solution.py:64
  120.5 1.2 copy-start.4
  121.7 1.2 copy-start.10
  134.7 11.6 %collective-permute-start.18 = (s16[2,672,128]{2,1,0:T(8,128)(2,1)}, s16[2,672,128]{2,1,0:T(8,128)(2,1)S(1)}, u32[]{:S(2)}, u32[]{:S(2)}) collective-permute-start(s16[2,672,128]{2,1,0:T(8,128)(2,1)} %get-tuple-element.34), channel_id=1, source_target_pairs={{0,32},{1,33},{2,34},{3,35},{4,36},{5,37},{6,38},{7,39},{8,40},{9,... | collective-permute-start | bytes 1032200 | tf_op jit(solution)/shard_map/ppermute | solution.py:60
  136.2 17.5 %collective-permute-start.19 = (s16[2,672,128]{2,1,0:T(8,128)(2,1)S(1)}, s16[2,672,128]{2,1,0:T(8,128)(2,1)S(1)}, u32[]{:S(2)}, u32[]{:S(2)}) collective-permute-start(s16[2,672,128]{2,1,0:T(8,128)(2,1)S(1)} %get-tuple-element.33), channel_id=1, source_target_pairs={{0,64},{1,65},{2,66},{3,67},{4,68},{5,69},{6,70},{7,71},{8,72},{9,... | collective-permute-start | bytes 1032200 | tf_op jit(solution)/shard_map/ppermute | solution.py:60
  138.6 15.1 %collective-permute-start.20 = (s16[2,672,128]{2,1,0:T(8,128)(2,1)S(1)}, s16[2,672,128]{2,1,0:T(8,128)(2,1)S(1)}, u32[]{:S(2)}, u32[]{:S(2)}) collective-permute-start(s16[2,672,128]{2,1,0:T(8,128)(2,1)S(1)} %get-tuple-element.32), channel_id=1, source_target_pairs={{0,96},{1,97},{2,98},{3,99},{4,100},{5,101},{6,102},{7,103},{8,104... | collective-permute-start | bytes 1032200 | tf_op jit(solution)/shard_map/ppermute | solution.py:60
